TPU v7x, 256 devices: a whole 4x4x8 slice. The times are simulated.
256 devices in a mesh: tensor: 4 (over y_hi, core), dp: 8 (over z), replica: 8 (over x, y_lo).
Axes of the slice: x: 4, y: 4 (y_hi: 2, y_lo: 2; y = y_hi * 2 + y_lo), z: 8, core: 2. Of those that a mesh axis runs over, the one named last changes fastest.
Arguments:
- features: bfloat16 [49152, 8192], P(('dp', 'replica'), 'tensor'), may hold values from -130 to 130
- cotangent: bfloat16 [49152, 1024], P(('dp', 'replica'), 'tensor'), may hold values from -45 to 45
- master: float32 [8192, 1024], P('dp', 'tensor'), may hold values from -6 to 6
- first: float32 [8192, 1024], P('dp', 'tensor'), may hold values from -3 to 3
- second: float32 [8192, 1024], P('dp', 'tensor'), may hold values from 0.05 to 2
Outputs:
- new_master: float32 [8192, 1024], P('dp', 'tensor')
- new_first: float32 [8192, 1024], P('dp', 'tensor')
- new_second: float32 [8192, 1024], P('dp', 'tensor')
All inputs are finite; a program needn't handle non-finite values.
Results may differ from a plain program's by a relative error of at most 0.0003.
Values may be sent and summed in bfloat16 or wider, within the bound.
No kernel may reach another device: no remote copies, remote signals or barrier semaphores. Data moves between devices by JAX's collectives and lax.ppermute only.
A program may use at most 128 MiB of HBM per device.

v0:
```python
import jax
import jax.numpy as jnp
from jax import lax
from jax.sharding import PartitionSpec as P

D = 8192


beta_one = 0.9
beta_two = 0.95
bias_first = 1.0 - 0.9**20
bias_second = 1.0 - 0.95**20
adam_eps = 1e-08
norm_eps = 1e-06
clip_level = 1.0
learn_rate = 0.01
weight_decay = 0.1


def contract_tokens(left, right):
    return lax.dot_general(
        left, right, (((0,), (0,)), ((), ())), preferred_element_type=jnp.float32
    )


def body(features, cotangent, master, first, second):
    width = lax.axis_size("tensor")
    total_cols = cotangent.shape[1] * width
    all_cols = lax.all_gather(cotangent, "tensor", axis=1, tiled=True)
    partial_rows = contract_tokens(features, all_cols)
    own_heads = lax.all_to_all(partial_rows, "tensor", split_axis=1, concat_axis=0, tiled=True)
    fine_part = lax.psum_scatter(own_heads, ("dp", "replica"), scatter_dimension=0, tiled=True)
    square_sum = lax.psum(jnp.sum(fine_part * fine_part), ("tensor", "dp", "replica"))
    grad = lax.all_gather(fine_part, "replica", axis=0, tiled=True)
    mean_square = square_sum / (D * total_cols)
    clip = jnp.minimum(1.0, clip_level / jnp.sqrt(mean_square + norm_eps))
    clipped = clip * grad
    new_first = beta_one * first + (1.0 - beta_one) * clipped
    new_second = beta_two * second + (1.0 - beta_two) * clipped * clipped
    update = new_first / bias_first / (jnp.sqrt(new_second / bias_second) + adam_eps)
    new_master = master - learn_rate * (update + weight_decay * master)
    return (new_master, new_first, new_second)


def solution(mesh):
    in_specs = (
        P(("dp", "replica"), "tensor"),
        P(("dp", "replica"), "tensor"),
        P("dp", "tensor"),
        P("dp", "tensor"),
        P("dp", "tensor"),
    )
    out_specs = (P("dp", "tensor"), P("dp", "tensor"), P("dp", "tensor"))
    return jax.shard_map(body, mesh=mesh, in_specs=in_specs, out_specs=out_specs, check_vma=False)
```

profile of v0, /device:TPU:1, one launch (start us, length us, event | category | flops | bytes accessed | tf_op | source)
XLA Modules:
  0.0 570.0 jit_solution(40635727126638985)
XLA Ops:
  7.2 0.0 copy-start
  7.2 0.0 all-gather.3.cloned.1.call-start
  7.2 0.7 all-gather.3.cloned.1.call-update
  7.9 0.0 reduce-scatter.2.cloned.1.call-start
  8.0 32.6 %all-gather.3.cloned.1.call-done = bf16[768,1024]{1,0:T(8,128)(2,1)} async-done(((bf16[768,256]{1,0:T(8,128)(2,1)}), bf16[768,1024]{1,0:T(8,128)(2,1)}) %all-gather.3.cloned.1.call-update) | async-done | bytes 1572880 | tf_op jit(solution)/shard_map/all_gather | solution.py:29
  40.5 0.0 copy-done
  40.5 4.9 fusion.2
  45.4 97.6 %all_to_all.19 = f32[2048,4,256]{0,2,1:T(8,128)} all-to-all(f32[2048,4,256]{0,2,1:T(8,128)S(1)} %bitcast.7), channel_id=1, replica_groups=mesh['tensor'=4,'dp'=8,'replica'=8] {'tensor'}, dimensions={1} | all-to-all | bytes 16777216 | tf_op jit(solution)/shard_map/all_to_all | solution.py:31
  143.1 8.7 %copy.8 = f32[4,2048,256]{2,1,0:T(8,128)} copy(f32[4,2048,256]{1,2,0:T(8,128)} %bitcast.6) | data formatting | bytes 16777216 | tf_op jit(solution)/shard_map/all_to_all | solution.py:31
  151.8 0.0 reduce-scatter.2.cloned.1.call-update
  151.8 0.0 all-gather.5.cloned.1.call-start
  151.8 285.3 %reduce-scatter.2.cloned.1.call-done = f32[128,256]{1,0:T(8,128)} async-done(((f32[8192,256]{1,0:T(8,128)}), f32[128,256]{1,0:T(8,128)}) %reduce-scatter.2.cloned.1.call-update) | async-done | bytes 131088 | tf_op jit(solution)/shard_map/reduce_scatter | solution.py:32
  437.1 0.0 all-gather.5.cloned.1.call-update
  437.1 1.5 multiply_reduce_fusion
  438.7 119.7 %psum.7 = f32[]{:T(128)} all-reduce(f32[]{:T(128)} %multiply_reduce_fusion), channel_id=1, replica_groups=mesh['tensor'=4,'dp'=8,'replica'=8] {'tensor','dp','replica'}, use_global_device_ids=true, to_apply=%region_2.0 | all-reduce | flops 1 | bytes 8 | tf_op jit(solution)/shard_map/psum | solution.py:33
  559.1 0.0 all-gather.5.cloned.1.call-done
  559.1 4.3 multiply_subtract_fusion
Async XLA Ops:
  7.2 33.4 %copy-start = (bf16[768,2048]{1,0:T(8,128)(2,1)S(1)}, bf16[768,2048]{1,0:T(8,128)(2,1)}, u32[]{:S(2)}) copy-start(bf16[768,2048]{1,0:T(8,128)(2,1)} %param.5) | copy-start | bytes 9437188
  7.2 33.4 %all-gather.3.cloned.1.call-start = ((), (), s32[]{:S(2)}) async-start(), calls=%async_computation.2 | async-start | bytes 1966080 | tf_op jit(solution)/shard_map/all_gather | solution.py:29
  7.9 429.2 %reduce-scatter.2.cloned.1.call-start = ((), (), s32[]{:S(2)}) async-start(), calls=%async_computation.3 | async-start | bytes 8519680 | tf_op jit(solution)/shard_map/reduce_scatter | solution.py:32
  151.8 407.3 %all-gather.5.cloned.1.call-start = ((), (), s32[]{:S(2)}) async-start(), calls=%async_computation.4 | async-start | bytes 1179648 | tf_op jit(solution)/shard_map/all_gather | solution.py:34
Sparse Core Ops, SparseCore 0:
  9.8 30.6 all-gather.2
  151.9 285.1 reduce-scatter.1
  438.9 80.3 all-gather.4
where the time goes:
time: 570 us
  waiting for transfers between devices  319 us (56%)
  blocking collectives  217 us (38%)
  between operations  14.5 us (3%)
  local copies, waits for them, and re-layouts  8.71 us (2%)
  other arithmetic  5.89 us (1%)
    reduce_scatter x1, waiting for transfers between devices, body(): lax.psum_scatter(own_heads, ('dp', 'replica'), scatter_dimension=0, tiled...  285 us
    psum x1, blocking collectives, body(): lax.psum(jnp.sum(fine_part * fine_part), ('tensor', 'dp', 'replica'))  120 us
    all_to_all x1, blocking collectives, body(): lax.all_to_all(partial_rows, 'tensor', split_axis=1, concat_axis=0, tiled...  97.6 us
    all_gather x1, waiting for transfers between devices, body(): all_cols = lax.all_gather(cotangent, 'tensor', axis=1, tiled=True)  32.6 us
  transfers between devices with their start and end apart: 3, of which 2 were waited for; matrix products, arithmetic and copies ran while one was open for 0% of the time, Pallas kernels for 0%

commit v1 on v0

--- a/solution.py
+++ b/solution.py
@@ -4,7 +4,6 @@
 from jax.sharding import PartitionSpec as P
 
 D = 8192
-
 
 beta_one = 0.9
 beta_two = 0.95
@@ -16,6 +15,10 @@
 learn_rate = 0.01
 weight_decay = 0.1
 
+EVERY = ("tensor", "dp", "replica")
+LINK = jnp.float16
+LINK_TOP = 60000.0
+
 
 def contract_tokens(left, right):
     return lax.dot_general(
@@ -23,15 +26,56 @@
     )
 
 
+def swap(x, axis):
+    return lax.all_to_all(x, axis, split_axis=0, concat_axis=0, tiled=True)
+
+
+def spread(value, axis):
+    count = lax.axis_size(axis)
+    return swap(jnp.broadcast_to(value[None], (count, *value.shape)), axis)
+
+
+def link_scale(features, cotangent, tokens):
+    feat_top = jnp.max(jnp.abs(features)).astype(jnp.float32)
+    cot_top = jnp.max(jnp.abs(cotangent)).astype(jnp.float32)
+    lane = lax.broadcasted_iota(jnp.int32, (1, 128), 1)
+    tops = spread(jnp.where(lane == 0, feat_top, cot_top), EVERY)
+    tops = jnp.max(tops, axis=(0, 1))
+    bound = jnp.maximum(tops[0] * tops[1] * tokens, 1e-30)
+    return LINK_TOP / bound, bound / LINK_TOP
+
+
 def body(features, cotangent, master, first, second):
-    width = lax.axis_size("tensor")
-    total_cols = cotangent.shape[1] * width
+    tensor, dp, replica = (lax.axis_size(a) for a in EVERY)
+    cols = cotangent.shape[1]
+    total_cols = cols * tensor
+    rows = features.shape[1]
+    halves = dp // tensor
+    part = rows // halves // replica
+    down, up = link_scale(features, cotangent, features.shape[0] * dp * replica)
     all_cols = lax.all_gather(cotangent, "tensor", axis=1, tiled=True)
-    partial_rows = contract_tokens(features, all_cols)
-    own_heads = lax.all_to_all(partial_rows, "tensor", split_axis=1, concat_axis=0, tiled=True)
-    fine_part = lax.psum_scatter(own_heads, ("dp", "replica"), scatter_dimension=0, tiled=True)
-    square_sum = lax.psum(jnp.sum(fine_part * fine_part), ("tensor", "dp", "replica"))
-    grad = lax.all_gather(fine_part, "replica", axis=0, tiled=True)
+
+    partial = contract_tokens(features, all_cols) * down
+    partial = partial.astype(LINK).reshape(halves, replica, part, total_cols)
+    got = swap(partial.transpose(1, 0, 2, 3), "replica")
+    mine = jnp.sum(got.astype(jnp.float32), axis=0)
+    mine = mine.astype(LINK).reshape(halves, part, tensor, cols)
+    got = swap(mine.transpose(0, 2, 1, 3).reshape(dp, part, cols), "dp")
+    fine = jnp.sum(got.astype(jnp.float32), axis=0) * up
+
+    to_owner = [
+        (t * dp + h * tensor + c, c * dp + halves * t + h)
+        for t in range(tensor)
+        for h in range(halves)
+        for c in range(tensor)
+    ]
+    moved = lax.ppermute(fine, ("tensor", "dp"), to_owner)
+    squares = spread(jnp.broadcast_to(jnp.sum(fine * fine), (1, 128)), ("tensor", "dp"))
+    squares = jnp.broadcast_to(jnp.sum(squares, axis=(0, 1))[:1], (8, cols))
+    told = spread(jnp.concatenate([moved, squares], axis=0), "replica")
+    grad = told[:, :part].reshape(replica * part, cols)
+    square_sum = jnp.sum(told[:, part, 0])
+
     mean_square = square_sum / (D * total_cols)
     clip = jnp.minimum(1.0, clip_level / jnp.sqrt(mean_square + norm_eps))
     clipped = clip * grad

time: 570 us -> 178 us (0.31)
  waiting for transfers between devices: 319 us -> 16.2 us
  blocking collectives: 217 us -> 114 us
  starting transfers between devices: 0.12 us -> 9.45 us
  other arithmetic: 5.89 us -> 12 us
  local copies, waits for them, and re-layouts: 8.71 us -> 2.85 us
    reduce_scatter x1 -> x0, waiting for transfers between devices: 285 us -> none  [body(): lax.psum_scatter(own_heads, ('dp', 'replica'), scatter_dimension=0, tiled...]
    psum x1 -> x0, blocking collectives: 120 us -> none  [body(): lax.psum(jnp.sum(fine_part * fine_part), ('tensor', 'dp', 'replica'))]
    all_gather x1, waiting for transfers between devices: 32.6 us -> 0.02 us  [body(): all_cols = lax.all_gather(cotangent, 'tensor', axis=1, tiled=True)]
    all_to_all x1 -> x4, blocking collectives: 97.6 us -> 114 us  [swap(): return lax.all_to_all(x, axis, split_axis=0, concat_axis=0, tiled=True)]
    all_to_all x0 -> x1, waiting for transfers between devices: none -> 15.5 us  [swap(): return lax.all_to_all(x, axis, split_axis=0, concat_axis=0, tiled=True)]
    all_to_all x1 -> x0, local copies, waits for them, and re-layouts: 8.7 us -> none  [body(): lax.all_to_all(partial_rows, 'tensor', split_axis=1, concat_axis=0, tiled...]
  transfers between devices with their start and end apart: 3 -> 3, of which waited for: 2 -> 1; matrix products, arithmetic and copies ran while one was open for 0% -> 4% of each run, Pallas kernels for 0% -> 0%
where the time goes in v1:
time: 178 us; the launch traced here: 177 us
  blocking collectives  114 us (64%)
  between operations  17.5 us (10%)
  waiting for transfers between devices  16.2 us (9%)
  other arithmetic  12 us (7%)
  starting transfers between devices  9.45 us (5%)
  matrix products  5.13 us (3%)
  local copies, waits for them, and re-layouts  2.85 us (2%)
    all_to_all x4, blocking collectives, swap(): return lax.all_to_all(x, axis, split_axis=0, concat_axis=0, tiled=True)  114 us
    all_to_all x1, waiting for transfers between devices, swap(): return lax.all_to_all(x, axis, split_axis=0, concat_axis=0, tiled=True)  15.5 us
    dot_general x1, matrix products, contract_tokens(): lax.dot_general(left, right, (((0,), (0,)), ((), ())), preferred_element_...  5.13 us
    all_to_all x1, starting transfers between devices, swap(): return lax.all_to_all(x, axis, split_axis=0, concat_axis=0, tiled=True)  5.03 us
    ppermute x1, starting transfers between devices, body(): moved = lax.ppermute(fine, ('tensor', 'dp'), to_owner)  4.38 us
  transfers between devices with their start and end apart: 3, of which 1 were waited for; matrix products, arithmetic and copies ran while one was open for 4% of the time, Pallas kernels for 0%

profile of v1, /device:TPU:1, one launch (start us, length us, event | category | flops | bytes accessed | tf_op | source)
XLA Modules:
  0.0 177.2 jit_solution(4387207565833480495)
XLA Ops:
  7.2 0.7 all-gather.2.cloned.1.call-update
  7.9 1.9 %abs_reduce_fusion.1 = bf16[]{:T(256)} fusion(bf16[768,256]{1,0:T(8,128)(2,1)} %param.6), kind=kLoop, calls=%fused_computation.12 | loop fusion | flops 393215 | bytes 393218 | tf_op jit(solution)/shard_map/reduce_max | solution.py:40
  10.4 3.1 %abs_reduce_fusion = bf16[]{:T(256)} fusion(bf16[768,2048]{1,0:T(8,128)(2,1)} %param.5), kind=kLoop, calls=%fused_computation.3 | loop fusion | flops 3145727 | bytes 3145730 | tf_op jit(solution)/shard_map/reduce_max | solution.py:39
  14.2 28.2 %all_to_all.25 = f32[256,1,128]{2,1,0:T(1,128)S(1)} all-to-all(f32[256,1,128]{2,1,0:T(1,128)S(1)} %broadcast_in_dim.14), channel_id=1, replica_groups=mesh['tensor'=4,'dp'=8,'replica'=8] {'tensor','dp','replica'}, dimensions={0} | all-to-all | bytes 262144 | tf_op jit(solution)/shard_map/all_to_all | solution.py:30
  42.5 0.6 fusion.5
  44.4 5.1 %multiply_convert_fusion = f16[2048,1024]{1,0:T(8,128)(2,1)S(1)} fusion(bf16[768,2048]{1,0:T(8,128)(2,1)S(1)} %copy-done, bf16[768,1024]{1,0:T(8,128)(2,1)} %all-gather.2.cloned.1.call-done, f32[]{:T(128)} %bitcast.1), kind=kOutput, calls=%fused_computation.1 | convolution fusion | flops 3225419776 | bytes 8912900 | tf_op jit(solution)/shard_map/dot_general | solution.py:24
  49.6 1.3 copy.14
  50.9 51.1 %all_to_all.26 = f16[8,2,128,1024]{3,2,1,0:T(8,128)(2,1)S(1)} all-to-all(f16[8,2,128,1024]{3,2,1,0:T(8,128)(2,1)S(1)} %bitcast.20), channel_id=1, replica_groups=mesh['tensor'=4,'dp'=8,'replica'=8] {'replica'}, dimensions={0} | all-to-all | bytes 8388608 | tf_op jit(solution)/shard_map/all_to_all | solution.py:30
  101.9 1.1 convert_reduce_fusion
  103.0 0.1 convert_element_type.22
  103.1 0.1 fusion.4
  103.2 1.0 pad_maximum_fusion
  104.2 5.0 %all-to-all-start.2 = ((f16[8,128,256]{2,1,0:T(8,128)(2,1)}), f16[8,128,256]{2,1,0:T(8,128)(2,1)S(1)}, u32[]{:S(2)}, u32[]{:S(2)}) async-start(f16[8,128,256]{2,1,0:T(8,128)(2,1)} %bitcast.4), calls=%async_computation.2 | async-start | bytes 1048576 | tf_op jit(solution)/shard_map/all_to_all | solution.py:30
  109.2 15.5 %all-to-all-done.2 = f16[8,128,256]{2,1,0:T(8,128)(2,1)S(1)} async-done(((f16[8,128,256]{2,1,0:T(8,128)(2,1)}), f16[8,128,256]{2,1,0:T(8,128)(2,1)S(1)}, u32[]{:S(2)}, u32[]{:S(2)}) %all-to-all-start.2) | async-done | bytes 524320 | tf_op jit(solution)/shard_map/all_to_all | solution.py:30
  124.6 0.1 convert_reduce_fusion.1
  124.7 0.6 multiply_reduce_fusion
  125.4 4.4 %collective-permute-start = (f32[128,256]{1,0:T(8,128)S(1)}, f32[128,256]{1,0:T(8,128)S(1)}, u32[]{:S(2)}, u32[]{:S(2)}) collective-permute-start(f32[128,256]{1,0:T(8,128)S(1)} %get-tuple-element.7), channel_id=1, source_target_pairs={{0,0},{8,64},{16,128},{24,192},{32,8},{40,72},{48,136},{56,200},{6... | collective-permute-start | bytes 393224 | tf_op jit(solution)/shard_map/ppermute | solution.py:72
  129.8 0.7 broadcast_in_dim_broadcast_in_dim_broadcast_in_dim.3
  130.4 16.7 %all_to_all.27 = f32[32,1,128]{2,1,0:T(1,128)S(1)} all-to-all(f32[32,1,128]{2,1,0:T(1,128)S(1)} %broadcast_in_dim_broadcast_in_dim_broadcast_in_dim.3), channel_id=1, replica_groups=mesh['tensor'=4,'dp'=8,'replica'=8] {'tensor','dp'}, dimensions={0} | all-to-all | bytes 32768 | tf_op jit(solution)/shard_map/all_to_all | solution.py:30
  147.2 0.1 broadcast_in_dim.26
  147.3 18.1 %all_to_all.28 = f32[8,136,256]{2,1,0:T(8,128)S(1)} all-to-all(f32[8,136,256]{2,1,0:T(8,128)S(1)} %broadcast_in_dim.26), channel_id=1, replica_groups=mesh['tensor'=4,'dp'=8,'replica'=8] {'replica'}, dimensions={0} | all-to-all | bytes 2228224 | tf_op jit(solution)/shard_map/all_to_all | solution.py:30
  165.4 0.6 slice_reduce_fusion
  166.7 0.1 slice_multiply_fusion
  166.8 3.5 %multiply_subtract_fusion = (f32[1024,256]{1,0:T(8,128)}, f32[1024,256]{1,0:T(8,128)}, f32[1024,256]{1,0:T(8,128)}) fusion(f32[1024,256]{1,0:T(8,128)S(1)} %copy-done.1, f32[8,128,256]{2,1,0:T(8,128)S(1)} %slice_multiply_fusion, f32[1024,256]{1,0:T(8,128)S(1)} %copy-done.2, f32[1024,256]{1,0:T(8,128)} %param.9), kind=kLoop, calls=%fused_computation.9 | loop fusion | flops 3932160 | bytes 7340032 | tf_op jit(solution)/shard_map/sub | solution.py:85
  (14 shorter events, 0.3 us)
Async XLA Ops:
  7.2 37.3 %copy-start = (bf16[768,2048]{1,0:T(8,128)(2,1)S(1)}, bf16[768,2048]{1,0:T(8,128)(2,1)}, u32[]{:S(2)}) copy-start(bf16[768,2048]{1,0:T(8,128)(2,1)} %param.5) | copy-start | bytes 9437188
  7.2 37.2 %all-gather.2.cloned.1.call-start = ((), (), s32[]{:S(2)}) async-start(), calls=%async_computation.5 | async-start | bytes 1966080 | tf_op jit(solution)/shard_map/all_gather | solution.py:56
  104.2 20.5 %all-to-all-start.2 = ((f16[8,128,256]{2,1,0:T(8,128)(2,1)}), f16[8,128,256]{2,1,0:T(8,128)(2,1)S(1)}, u32[]{:S(2)}, u32[]{:S(2)}) async-start(f16[8,128,256]{2,1,0:T(8,128)(2,1)} %bitcast.4), calls=%async_computation.2 | async-start | bytes 1048576 | tf_op jit(solution)/shard_map/all_to_all | solution.py:30
  124.7 42.1 %copy-start.1 = (f32[1024,256]{1,0:T(8,128)S(1)}, f32[1024,256]{1,0:T(8,128)}, u32[]{:S(2)}) copy-start(f32[1024,256]{1,0:T(8,128)} %param.7) | copy-start | bytes 3145732
  124.7 42.1 %copy-start.2 = (f32[1024,256]{1,0:T(8,128)S(1)}, f32[1024,256]{1,0:T(8,128)}, u32[]{:S(2)}) copy-start(f32[1024,256]{1,0:T(8,128)} %param.8) | copy-start | bytes 3145732
  125.4 21.8 %collective-permute-start = (f32[128,256]{1,0:T(8,128)S(1)}, f32[128,256]{1,0:T(8,128)S(1)}, u32[]{:S(2)}, u32[]{:S(2)}) collective-permute-start(f32[128,256]{1,0:T(8,128)S(1)} %get-tuple-element.7), channel_id=1, source_target_pairs={{0,0},{8,64},{16,128},{24,192},{32,8},{40,72},{48,136},{56,200},{6... | collective-permute-start | bytes 393224 | tf_op jit(solution)/shard_map/ppermute | solution.py:72
Sparse Core Ops, SparseCore 0:
  9.8 31.7 all-gather.1

commit v2 on v0

--- a/solution.py
+++ b/solution.py
@@ -4,7 +4,6 @@
 from jax.sharding import PartitionSpec as P
 
 D = 8192
-
 
 beta_one = 0.9
 beta_two = 0.95
@@ -16,22 +15,78 @@
 learn_rate = 0.01
 weight_decay = 0.1
 
+EVERY = ("tensor", "dp", "replica")
+SUMMED = ("dp", "replica")
+LINK = jnp.float16
+LINK_TOP = 60000.0
+LEAST = 1e-30
+LANES = 128
+F32 = jnp.float32
+
 
 def contract_tokens(left, right):
     return lax.dot_general(
-        left, right, (((0,), (0,)), ((), ())), preferred_element_type=jnp.float32
+        left, right, (((0,), (0,)), ((), ())), preferred_element_type=F32
     )
 
 
+def swap(x, axis, groups=None):
+    return lax.all_to_all(x, axis, split_axis=0, concat_axis=0, axis_index_groups=groups, tiled=True)
+
+
+def spread(value, axis, count, groups=None):
+    return swap(jnp.broadcast_to(value[None], (count, *value.shape)), axis, groups)
+
+
+def partner(x, bit):
+    count = lax.axis_size("tensor")
+    return lax.ppermute(x, "tensor", [(i, i ^ bit) for i in range(count)])
+
+
+def top_of(x):
+    return jnp.max(jnp.abs(x)).astype(F32)
+
+
 def body(features, cotangent, master, first, second):
-    width = lax.axis_size("tensor")
-    total_cols = cotangent.shape[1] * width
-    all_cols = lax.all_gather(cotangent, "tensor", axis=1, tiled=True)
-    partial_rows = contract_tokens(features, all_cols)
-    own_heads = lax.all_to_all(partial_rows, "tensor", split_axis=1, concat_axis=0, tiled=True)
-    fine_part = lax.psum_scatter(own_heads, ("dp", "replica"), scatter_dimension=0, tiled=True)
-    square_sum = lax.psum(jnp.sum(fine_part * fine_part), ("tensor", "dp", "replica"))
-    grad = lax.all_gather(fine_part, "replica", axis=0, tiled=True)
+    tensor, dp, replica = (lax.axis_size(a) for a in EVERY)
+    tokens, rows = features.shape
+    cols = cotangent.shape[1]
+    total_cols = cols * tensor
+    halves = dp // tensor
+    part = rows // halves // replica
+    run = halves * replica
+    runs = [list(range(i * run, (i + 1) * run)) for i in range(tensor)]
+    blocks_of_runs = [[t * dp * replica + i for t in range(tensor) for i in r] for r in runs]
+    apart = [[i * halves + h for i in range(tensor)] for h in range(halves)]
+
+    columns = [cotangent] + [partner(cotangent, j) for j in range(1, tensor)]
+    columns = jnp.concatenate(columns, axis=1)
+
+    lane = lax.broadcasted_iota(jnp.int32, (1, LANES), 1)
+    tops = jnp.where(lane == 0, top_of(features), top_of(cotangent))
+    tops = jnp.max(spread(tops, EVERY, tensor * run, blocks_of_runs), axis=(0, 1))
+    bound = jnp.maximum(tops[0] * tops[1] * (tokens * run), LEAST)
+
+    partial = (contract_tokens(features, columns) * (LINK_TOP / bound)).astype(LINK)
+    got = swap(partial.reshape(run, part, total_cols), SUMMED, runs)
+    mine = jnp.sum(got.astype(F32), axis=0) * bound * (1.0 / LINK_TOP)
+    blocks = jnp.stack([mine[:, j * cols : (j + 1) * cols] for j in range(tensor)])
+    fine = jnp.sum(swap(blocks, "dp", apart), axis=0)
+
+    to_owner = [
+        (t * dp + j * halves + h, (t ^ j) * dp + t * halves + h)
+        for t in range(tensor)
+        for j in range(tensor)
+        for h in range(halves)
+    ]
+    moved = lax.ppermute(fine, ("tensor", "dp"), to_owner)
+    squares = jnp.broadcast_to(jnp.sum(fine * fine), (1, LANES))
+    squares = spread(squares, ("tensor", "dp"), tensor * dp)
+    squares = jnp.broadcast_to(jnp.sum(squares, axis=(0, 1))[:1], (8, cols))
+    told = spread(jnp.concatenate([moved, squares], axis=0), "replica", replica)
+    grad = told[:, :part].reshape(replica * part, cols)
+    square_sum = jnp.sum(told[:, part, 0])
+
     mean_square = square_sum / (D * total_cols)
     clip = jnp.minimum(1.0, clip_level / jnp.sqrt(mean_square + norm_eps))
     clipped = clip * grad

time: 570 us -> 160 us (0.28)
  waiting for transfers between devices: 319 us -> 0.01 us
  blocking collectives: 217 us -> 126 us
  starting transfers between devices: 0.12 us -> 11.6 us
  between operations: 14.5 us -> 4.17 us
  local copies, waits for them, and re-layouts: 8.71 us -> 2.54 us
    reduce_scatter x1 -> x0, waiting for transfers between devices: 285 us -> none  [body(): lax.psum_scatter(own_heads, ('dp', 'replica'), scatter_dimension=0, tiled...]
    psum x1 -> x0, blocking collectives: 120 us -> none  [body(): lax.psum(jnp.sum(fine_part * fine_part), ('tensor', 'dp', 'replica'))]
    all_gather x2 -> x0, waiting for transfers between devices: 32.6 us -> none  [the longest x1 32.6 us: body(): all_cols = lax.all_gather(cotangent, 'tensor', axis=1, tiled=True)]
    all_to_all x1 -> x5, blocking collectives: 97.6 us -> 126 us  [swap(): lax.all_to_all(x, axis, split_axis=0, concat_axis=0, axis_index_groups=gr...]
    ppermute x0 -> x4, starting transfers between devices: none -> 11.6 us  [the longest x3 6.19 us: partner(): return lax.ppermute(x, 'tensor', [(i, i ^ bit) for i in range(count)])]
    all_to_all x1 -> x0, local copies, waits for them, and re-layouts: 8.7 us -> none  [body(): lax.all_to_all(partial_rows, 'tensor', split_axis=1, concat_axis=0, tiled...]
  transfers between devices with their start and end apart: 3 -> 4, of which waited for: 2 -> 0; matrix products, arithmetic and copies ran while one was open for 0% -> 4% of each run, Pallas kernels for 0% -> 0%
where the time goes in v2:
time: 160 us; the launch traced here: 159 us
  blocking collectives  126 us (79%)
  starting transfers between devices  11.6 us (7%)
  other arithmetic  9.99 us (6%)
  matrix products  4.99 us (3%)
  between operations  4.17 us (3%)
  local copies, waits for them, and re-layouts  2.54 us (2%)
    all_to_all x5, blocking collectives, swap(): lax.all_to_all(x, axis, split_axis=0, concat_axis=0, axis_index_groups=gr...  126 us
    ppermute x3, starting transfers between devices, partner(): return lax.ppermute(x, 'tensor', [(i, i ^ bit) for i in range(count)])  6.19 us
    ppermute x1, starting transfers between devices, body(): moved = lax.ppermute(fine, ('tensor', 'dp'), to_owner)  5.43 us
    dot_general x1, matrix products, contract_tokens(): lax.dot_general(left, right, (((0,), (0,)), ((), ())), preferred_element_...  4.99 us
    reduce_max x2, other arithmetic, top_of(): return jnp.max(jnp.abs(x)).astype(F32)  3.71 us
    sub x1, other arithmetic, body(): new_master = master - learn_rate * (update + weight_decay * master)  3.47 us
  transfers between devices with their start and end apart: 4, of which 0 were waited for; matrix products, arithmetic and copies ran while one was open for 4% of the time, Pallas kernels for 0%

profile of v2, /device:TPU:1, one launch (start us, length us, event | category | flops | bytes accessed | tf_op | source)
XLA Modules:
  0.0 159.4 jit_solution(18048679919619521088)
XLA Ops:
  0.6 4.4 %collective-permute-start.2 = (bf16[768,256]{1,0:T(8,128)(2,1)}, bf16[768,256]{1,0:T(8,128)(2,1)}, u32[]{:S(2)}, u32[]{:S(2)}) collective-permute-start(bf16[768,256]{1,0:T(8,128)(2,1)} %param.6), channel_id=1, source_target_pairs={{0,192},{64,128},{128,64},{192,0},{1,193},{65,129},{129,65},{193,1... | collective-permute-start | bytes 1179656 | tf_op jit(solution)/shard_map/ppermute | solution.py:43
  5.0 1.8 %collective-permute-start.1 = (bf16[768,256]{1,0:T(8,128)(2,1)}, bf16[768,256]{1,0:T(8,128)(2,1)}, u32[]{:S(2)}, u32[]{:S(2)}) collective-permute-start(bf16[768,256]{1,0:T(8,128)(2,1)} %param.6), channel_id=1, source_target_pairs={{0,128},{64,192},{128,0},{192,64},{1,129},{65,193},{129,1},{193,65... | collective-permute-start | bytes 1179656 | tf_op jit(solution)/shard_map/ppermute | solution.py:43
  6.8 3.1 %abs_reduce_fusion = bf16[]{:T(256)} fusion(bf16[768,2048]{1,0:T(8,128)(2,1)} %param.5), kind=kLoop, calls=%fused_computation.3 | loop fusion | flops 3145727 | bytes 3145730 | tf_op jit(solution)/shard_map/reduce_max | solution.py:47
  9.9 0.7 abs_reduce_fusion.1
  11.9 15.1 %all_to_all.25 = f32[64,1,128]{2,1,0:T(1,128)} all-to-all(f32[64,1,128]{2,1,0:T(1,128)S(1)} %broadcast_in_dim.14), channel_id=1, replica_groups={{0,1,2,3,4,5,6,7,8,9,10,11,12,13,14,15,64,65,66,67,68,69,70,71,72,73,74..., dimensions={0} | all-to-all | bytes 65536 | tf_op jit(solution)/shard_map/all_to_all | solution.py:34
  27.0 0.8 reduce_max.29
  27.8 0.6 fusion.13
  29.8 5.0 %fusion = f16[128,16,8,128]{3,2,1,0:T(8,128)(2,1)S(1)} fusion(f32[]{:T(128)S(6)} %div.22, bf16[768,2048]{1,0:T(8,128)(2,1)S(1)} %copy-done, bf16[768,256]{1,0:T(8,128)(2,1)} %collective-permute-done.2, bf16[768,256]{1,0:T(8,128)(2,1)} %collective-permute-done.1, bf16[768,256]{1,0:T(8,128)(2,1)} %collective-permute-done, bf16[768,256]{1,0:T(8,128)(2,1)S(1)} %copy-done.3), kind=kOutput, calls=%fused_computation.4 | convolution fusion | flops 3231711232 | bytes 8912900 | tf_op jit(solution)/shard_map/dot_general | solution.py:28
  34.8 1.0 copy.25
  35.8 52.4 %all_to_all.26 = f16[16,128,1024]{1,2,0:T(8,128)(2,1)S(1)} all-to-all(f16[16,128,1024]{1,2,0:T(8,128)(2,1)S(1)} %bitcast.27), channel_id=1, replica_groups={{0,1,2,3,4,5,6,7,8,9,10,11,12,13,14,15},{16,17,18,19,20,21,22,23,24,25,..., dimensions={0} | all-to-all | bytes 8388608 | tf_op jit(solution)/shard_map/all_to_all | solution.py:34
  88.1 0.6 convert_reduce_fusion
  88.7 0.1 multiply_multiply_fusion.1
  88.9 21.6 %all_to_all.27 = f32[4,128,256]{1,2,0:T(8,128)S(1)} all-to-all(f32[4,128,256]{1,2,0:T(8,128)S(1)} %pad_maximum_fusion), channel_id=1, replica_groups={{0,16,32,48},{8,24,40,56},{1,17,33,49},{9,25,41,57},{2,18,34,50},{10,26..., dimensions={0} | all-to-all | bytes 1048576 | tf_op jit(solution)/shard_map/all_to_all | solution.py:34
  110.5 0.0 copy-start.1
  110.5 5.4 %collective-permute-start.3 = (f32[128,256]{0,1:T(8,128)S(1)}, f32[128,256]{0,1:T(8,128)S(1)}, u32[]{:S(2)}, u32[]{:S(2)}) collective-permute-start(f32[128,256]{0,1:T(8,128)S(1)} %reduce_sum.46), channel_id=1, source_target_pairs={{0,0},{8,8},{16,64},{24,72},{32,128},{40,136},{48,192},{56,200},{6... | collective-permute-start | bytes 393224 | tf_op jit(solution)/shard_map/ppermute | solution.py:82
  116.0 0.6 multiply_reduce_fusion
  116.6 0.7 broadcast_in_dim_broadcast_in_dim_broadcast_in_dim.3
  117.3 18.0 %all_to_all.28 = f32[32,1,128]{2,1,0:T(1,128)S(1)} all-to-all(f32[32,1,128]{2,1,0:T(1,128)S(1)} %broadcast_in_dim_broadcast_in_dim_broadcast_in_dim.3), channel_id=1, replica_groups=mesh['tensor'=4,'dp'=8,'replica'=8] {'tensor','dp'}, dimensions={0} | all-to-all | bytes 32768 | tf_op jit(solution)/shard_map/all_to_all | solution.py:34
  135.3 0.1 copy.22
  135.5 0.1 broadcast_in_dim.26
  135.6 19.0 %all_to_all.29 = f32[8,136,256]{2,1,0:T(8,128)S(1)} all-to-all(f32[8,136,256]{2,1,0:T(8,128)S(1)} %broadcast_in_dim.26), channel_id=1, replica_groups=mesh['tensor'=4,'dp'=8,'replica'=8] {'replica'}, dimensions={0} | all-to-all | bytes 2228224 | tf_op jit(solution)/shard_map/all_to_all | solution.py:34
  154.6 0.6 slice_reduce_fusion
  155.9 0.1 slice_multiply_fusion
  156.0 3.5 %multiply_subtract_fusion = (f32[1024,256]{1,0:T(8,128)}, f32[1024,256]{1,0:T(8,128)}, f32[1024,256]{1,0:T(8,128)}) fusion(f32[1024,256]{1,0:T(8,128)S(1)} %copy-done.1, f32[8,128,256]{2,1,0:T(8,128)S(1)} %slice_multiply_fusion, f32[1024,256]{1,0:T(8,128)S(1)} %copy-done.2, f32[1024,256]{1,0:T(8,128)} %param.9), kind=kLoop, calls=%fused_computation.17 | loop fusion | flops 3932160 | bytes 7340032 | tf_op jit(solution)/shard_map/sub | solution.py:96
  (19 shorter events, 0.2 us)
Async XLA Ops:
  0.6 9.3 %copy-start.3 = (bf16[768,256]{1,0:T(8,128)(2,1)S(1)}, bf16[768,256]{1,0:T(8,128)(2,1)}, u32[]{:S(2)}) copy-start(bf16[768,256]{1,0:T(8,128)(2,1)} %param.6) | copy-start | bytes 1179652
  0.6 29.1 %copy-start = (bf16[768,2048]{1,0:T(8,128)(2,1)S(1)}, bf16[768,2048]{1,0:T(8,128)(2,1)}, u32[]{:S(2)}) copy-start(bf16[768,2048]{1,0:T(8,128)(2,1)} %param.5) | copy-start | bytes 9437188
  0.6 29.1 %collective-permute-start.2 = (bf16[768,256]{1,0:T(8,128)(2,1)}, bf16[768,256]{1,0:T(8,128)(2,1)}, u32[]{:S(2)}, u32[]{:S(2)}) collective-permute-start(bf16[768,256]{1,0:T(8,128)(2,1)} %param.6), channel_id=1, source_target_pairs={{0,192},{64,128},{128,64},{192,0},{1,193},{65,129},{129,65},{193,1... | collective-permute-start | bytes 1179656 | tf_op jit(solution)/shard_map/ppermute | solution.py:43
  5.0 24.7 %collective-permute-start.1 = (bf16[768,256]{1,0:T(8,128)(2,1)}, bf16[768,256]{1,0:T(8,128)(2,1)}, u32[]{:S(2)}, u32[]{:S(2)}) collective-permute-start(bf16[768,256]{1,0:T(8,128)(2,1)} %param.6), channel_id=1, source_target_pairs={{0,128},{64,192},{128,0},{192,64},{1,129},{65,193},{129,1},{193,65... | collective-permute-start | bytes 1179656 | tf_op jit(solution)/shard_map/ppermute | solution.py:43
  6.8 22.9 %collective-permute-start = (bf16[768,256]{1,0:T(8,128)(2,1)}, bf16[768,256]{1,0:T(8,128)(2,1)}, u32[]{:S(2)}, u32[]{:S(2)}) collective-permute-start(bf16[768,256]{1,0:T(8,128)(2,1)} %param.6), channel_id=1, source_target_pairs={{0,64},{64,0},{128,192},{192,128},{1,65},{65,1},{129,193},{193,129... | collective-permute-start | bytes 1179656 | tf_op jit(solution)/shard_map/ppermute | solution.py:43
  110.5 45.4 %copy-start.1 = (f32[1024,256]{1,0:T(8,128)S(1)}, f32[1024,256]{1,0:T(8,128)}, u32[]{:S(2)}) copy-start(f32[1024,256]{1,0:T(8,128)} %param.7) | copy-start | bytes 3145732
  110.5 45.4 %copy-start.2 = (f32[1024,256]{1,0:T(8,128)S(1)}, f32[1024,256]{1,0:T(8,128)}, u32[]{:S(2)}) copy-start(f32[1024,256]{1,0:T(8,128)} %param.8) | copy-start | bytes 3145732
  110.5 24.8 %collective-permute-start.3 = (f32[128,256]{0,1:T(8,128)S(1)}, f32[128,256]{0,1:T(8,128)S(1)}, u32[]{:S(2)}, u32[]{:S(2)}) collective-permute-start(f32[128,256]{0,1:T(8,128)S(1)} %reduce_sum.46), channel_id=1, source_target_pairs={{0,0},{8,8},{16,64},{24,72},{32,128},{40,136},{48,192},{56,200},{6... | collective-permute-start | bytes 393224 | tf_op jit(solution)/shard_map/ppermute | solution.py:82

commit v3 on v2

--- a/solution.py
+++ b/solution.py
@@ -1,6 +1,11 @@
+import functools
+import math
+
 import jax
 import jax.numpy as jnp
 from jax import lax
+from jax.experimental import pallas as pl
+from jax.experimental.pallas import tpu as pltpu
 from jax.sharding import PartitionSpec as P
 
 D = 8192
@@ -21,7 +26,10 @@
 LINK_TOP = 60000.0
 LEAST = 1e-30
 LANES = 128
+TOLD = 8
 F32 = jnp.float32
+SMALL = pltpu.CompilerParams(vmem_limit_bytes=4 * 2**20)
+WHOLE = pl.BlockSpec(memory_space=pltpu.VMEM)
 
 
 def contract_tokens(left, right):
@@ -43,8 +51,88 @@
     return lax.ppermute(x, "tensor", [(i, i ^ bit) for i in range(count)])
 
 
-def top_of(x):
-    return jnp.max(jnp.abs(x)).astype(F32)
+def tops_kernel(features_ref, cotangent_ref, out_ref):
+    feat_top = jnp.max(jnp.max(jnp.abs(features_ref[...]).reshape(-1, 16, features_ref.shape[1]), axis=0).astype(F32))
+    cot_top = jnp.max(jnp.max(jnp.abs(cotangent_ref[...]).reshape(-1, 16, cotangent_ref.shape[1]), axis=0).astype(F32))
+    lane = lax.broadcasted_iota(jnp.int32, out_ref.shape, 2)
+    out_ref[...] = jnp.where(lane == 0, feat_top, cot_top)
+
+
+def tops_of(features, cotangent, count):
+    return pl.pallas_call(
+        tops_kernel,
+        in_specs=[WHOLE] * 2,
+        out_specs=WHOLE,
+        out_shape=jax.ShapeDtypeStruct((count, 1, LANES), F32),
+        compiler_params=pltpu.CompilerParams(vmem_limit_bytes=16 * 2**20),
+        cost_estimate=pl.CostEstimate(flops=2 * features.size, bytes_accessed=2 * features.size, transcendentals=0),
+        name="tops",
+    )(features, cotangent)
+
+
+def scale_kernel(terms, tops_ref, down_ref, exponent_ref):
+    tops = jnp.max(tops_ref[...], axis=0)
+    lane = lax.broadcasted_iota(jnp.int32, tops.shape, 1)
+    feat_top = jnp.max(jnp.where(lane == 0, tops, 0.0))
+    cot_top = jnp.max(jnp.where(lane == 0, 0.0, tops))
+    bound = jnp.maximum(jnp.full((8, LANES), feat_top) * cot_top * terms, LEAST)
+    exponent = jnp.ceil(jnp.log2(bound * (1.0 / LINK_TOP)))
+    down_ref[...] = jnp.exp2(-exponent)[:1, :1]
+    exponent_ref[...] = exponent[:1, :1]
+
+
+def scale_for(tops, terms):
+    one = jax.ShapeDtypeStruct((1, 1), F32)
+    down, exponent = pl.pallas_call(
+        functools.partial(scale_kernel, terms),
+        in_specs=[WHOLE],
+        out_specs=[WHOLE] * 2,
+        out_shape=[one, one],
+        compiler_params=SMALL,
+        name="scale",
+    )(tops)
+    return down.reshape(()), exponent.reshape(())
+
+
+def squares_kernel(fine_ref, out_ref):
+    out_ref[...] = jnp.full(out_ref.shape, jnp.sum(fine_ref[...] * fine_ref[...]))
+
+
+def squares_of(fine, count):
+    return pl.pallas_call(
+        squares_kernel,
+        in_specs=[WHOLE],
+        out_specs=WHOLE,
+        out_shape=jax.ShapeDtypeStruct((count, 1, LANES), F32),
+        compiler_params=SMALL,
+        name="squares",
+    )(fine)
+
+
+def pack_kernel(moved_ref, squares_ref, out_ref):
+    cols, part = moved_ref.shape
+    total = jnp.sum(squares_ref[...], axis=0)
+    total = jnp.maximum(jnp.concatenate([total] * (cols // LANES), axis=1), LEAST)
+    exponent = jnp.ceil(0.5 * jnp.log2(total) - math.log2(LINK_TOP))
+    scale = jnp.exp2(-exponent)
+    level = total * scale * scale * LINK_TOP**-2
+    high = jnp.floor(level * 2048.0) * (1.0 / 2048.0)
+    low = (level - high) * 2048.0
+    row = lax.broadcasted_iota(jnp.int32, (TOLD, cols), 0)
+    out_ref[:part] = moved_ref[...].T * scale
+    out_ref[part:] = jnp.where(row == 0, exponent, jnp.where(row == 1, high, low))
+
+
+def pack(moved, squares):
+    cols, part = moved.shape
+    return pl.pallas_call(
+        pack_kernel,
+        in_specs=[WHOLE] * 2,
+        out_specs=WHOLE,
+        out_shape=jax.ShapeDtypeStruct((part + TOLD, cols), F32),
+        compiler_params=SMALL,
+        name="pack",
+    )(moved, squares)
 
 
 def body(features, cotangent, master, first, second):
@@ -62,16 +150,16 @@
     columns = [cotangent] + [partner(cotangent, j) for j in range(1, tensor)]
     columns = jnp.concatenate(columns, axis=1)
 
-    lane = lax.broadcasted_iota(jnp.int32, (1, LANES), 1)
-    tops = jnp.where(lane == 0, top_of(features), top_of(cotangent))
-    tops = jnp.max(spread(tops, EVERY, tensor * run, blocks_of_runs), axis=(0, 1))
-    bound = jnp.maximum(tops[0] * tops[1] * (tokens * run), LEAST)
+    tops = swap(tops_of(features, cotangent, tensor * run), EVERY, blocks_of_runs)
+    down, exponent = scale_for(tops, tokens * run)
 
-    partial = (contract_tokens(features, columns) * (LINK_TOP / bound)).astype(LINK)
-    got = swap(partial.reshape(run, part, total_cols), SUMMED, runs)
-    mine = jnp.sum(got.astype(F32), axis=0) * bound * (1.0 / LINK_TOP)
-    blocks = jnp.stack([mine[:, j * cols : (j + 1) * cols] for j in range(tensor)])
-    fine = jnp.sum(swap(blocks, "dp", apart), axis=0)
+    partial = (contract_tokens(columns, features) * down).astype(LINK)
+    partial = partial.reshape(total_cols, run, part).transpose(1, 0, 2)
+    mine = jnp.sum(swap(partial, SUMMED, runs).astype(F32), axis=0).reshape(tensor, cols, part)
+    note = exponent + 0.0 * mine[:, :TOLD]
+    message = jnp.concatenate([mine, note], axis=1).astype(LINK)
+    got = swap(message, "dp", apart).astype(F32)
+    fine = jnp.sum(got[:, :cols] * jnp.exp2(got[:, cols : cols + 1]), axis=0)
 
     to_owner = [
         (t * dp + j * halves + h, (t ^ j) * dp + t * halves + h)
@@ -80,12 +168,12 @@
         for h in range(halves)
     ]
     moved = lax.ppermute(fine, ("tensor", "dp"), to_owner)
-    squares = jnp.broadcast_to(jnp.sum(fine * fine), (1, LANES))
-    squares = spread(squares, ("tensor", "dp"), tensor * dp)
-    squares = jnp.broadcast_to(jnp.sum(squares, axis=(0, 1))[:1], (8, cols))
-    told = spread(jnp.concatenate([moved, squares], axis=0), "replica", replica)
-    grad = told[:, :part].reshape(replica * part, cols)
-    square_sum = jnp.sum(told[:, part, 0])
+    squares = swap(squares_of(fine, tensor * dp), ("tensor", "dp"))
+    told = spread(pack(moved, squares).astype(LINK), "replica", replica).astype(F32)
+    factors = jnp.exp2(told[:, part : part + 1])
+    halfway = told[:, part + 1 : part + 2] + told[:, part + 2 : part + 3] * (1.0 / 2048.0)
+    square_sum = jnp.sum(halfway * factors * factors, axis=0) * LINK_TOP**2
+    grad = (told[:, :part] * factors).reshape(replica * part, cols)
 
     mean_square = square_sum / (D * total_cols)
     clip = jnp.minimum(1.0, clip_level / jnp.sqrt(mean_square + norm_eps))

time: 160 us -> 143 us (0.89)
  blocking collectives: 126 us -> 118 us
  other arithmetic: 9.99 us -> 3.83 us
  between operations: 4.17 us -> 0.84 us
  starting transfers between devices: 11.6 us -> 9.67 us
    all_to_all x5, blocking collectives: 126 us -> 118 us  [swap(): lax.all_to_all(x, axis, split_axis=0, concat_axis=0, axis_index_groups=gr...]
    reduce_max x3 -> x0, other arithmetic: 4.49 us -> none  [the longest x2 3.71 us: top_of(): return jnp.max(jnp.abs(x)).astype(F32)]
    unnamed x9 -> x15, local copies, waits for them, and re-layouts: 0.12 us -> 2.91 us
    ppermute x1, starting transfers between devices: 5.43 us -> 3.49 us  [body(): moved = lax.ppermute(fine, ('tensor', 'dp'), to_owner)]
  transfers between devices with their start and end apart: 4 -> 4, of which waited for: 0 -> 0; matrix products, arithmetic and copies ran while one was open for 4% -> 0% of each run, Pallas kernels for 0% -> 1%
where the time goes in v3:
time: 143 us
  blocking collectives  118 us (83%)
  starting transfers between devices  9.67 us (7%)
  matrix products  4.73 us (3%)
  local copies, waits for them, and re-layouts  3.96 us (3%)
  other arithmetic  3.83 us (3%)
    all_to_all x5, blocking collectives, swap(): lax.all_to_all(x, axis, split_axis=0, concat_axis=0, axis_index_groups=gr...  118 us
    ppermute x3, starting transfers between devices, partner(): return lax.ppermute(x, 'tensor', [(i, i ^ bit) for i in range(count)])  6.19 us
    dot_general x1, matrix products, contract_tokens(): lax.dot_general(left, right, (((0,), (0,)), ((), ())), preferred_element_...  4.73 us
    ppermute x1, starting transfers between devices, body(): moved = lax.ppermute(fine, ('tensor', 'dp'), to_owner)  3.49 us
    unnamed x15, local copies, waits for them, and re-layouts  2.91 us
  transfers between devices with their start and end apart: 4, of which 0 were waited for; matrix products, arithmetic and copies ran while one was open for 0% of the time, Pallas kernels for 1%

profile of v3, /device:TPU:1, one launch (start us, length us, event | category | flops | bytes accessed | tf_op | source)
XLA Modules:
  0.0 142.6 jit_solution(14893011535560427327)
XLA Ops:
  0.6 4.4 %collective-permute-start.2 = (bf16[768,256]{1,0:T(8,128)(2,1)}, bf16[768,256]{1,0:T(8,128)(2,1)S(1)}, u32[]{:S(2)}, u32[]{:S(2)}) collective-permute-start(bf16[768,256]{1,0:T(8,128)(2,1)} %cotangent_ref.1), channel_id=1, source_target_pairs={{0,192},{64,128},{128,64},{192,0},{1,193},{65,129},{129,65},{193,1... | collective-permute-start | bytes 1179656 | tf_op jit(solution)/shard_map/ppermute | solution.py:51
  5.0 1.8 %collective-permute-start.1 = (bf16[768,256]{1,0:T(8,128)(2,1)}, bf16[768,256]{1,0:T(8,128)(2,1)S(1)}, u32[]{:S(2)}, u32[]{:S(2)}) collective-permute-start(bf16[768,256]{1,0:T(8,128)(2,1)} %cotangent_ref.1), channel_id=1, source_target_pairs={{0,128},{64,192},{128,0},{192,64},{1,129},{65,193},{129,1},{193,65... | collective-permute-start | bytes 1179656 | tf_op jit(solution)/shard_map/ppermute | solution.py:51
  6.8 1.9 %copy-done = bf16[768,2048]{1,0:T(8,128)(2,1)S(1)} copy-done((bf16[768,2048]{1,0:T(8,128)(2,1)S(1)}, bf16[768,2048]{1,0:T(8,128)(2,1)}, u32[]{:S(2)}) %copy-start) | copy-done | bytes 3145752
  8.7 1.0 copy-done.2
  9.7 0.3 tops.1
  10.0 15.3 %all_to_all.25.tops_ref = f32[64,1,128]{2,1,0:T(1,128)S(1)} all-to-all(f32[64,1,128]{2,1,0:T(1,128)S(1)} %tops.1), channel_id=1, replica_groups={{0,1,2,3,4,5,6,7,8,9,10,11,12,13,14,15,64,65,66,67,68,69,70,71,72,73,74..., dimensions={0} | all-to-all | bytes 65536 | tf_op jit(solution)/shard_map/all_to_all | solution.py:42
  25.3 0.7 scale.1
  26.0 4.7 %fusion = f16[128,16,8,128]{3,2,1,0:T(8,128)(2,1)S(1)} fusion(f32[]{:T(128)} %bitcast, bf16[768,2048]{1,0:T(8,128)(2,1)S(1)} %copy-done.1, bf16[768,256]{1,0:T(8,128)(2,1)S(1)} %collective-permute-done.2, bf16[768,256]{1,0:T(8,128)(2,1)S(1)} %collective-permute-done.1, bf16[768,256]{1,0:T(8,128)(2,1)S(1)} %collective-permute-done, ...), kind=kOutput, calls=%fused_computation.3 | convolution fusion | flops 3231711232 | bytes 8912900 | tf_op jit(solution)/shard_map/dot_general | solution.py:36
  30.7 1.0 copy.14
  31.7 54.0 %all_to_all.26 = f16[16,1024,128]{2,1,0:T(8,128)(2,1)S(1)} all-to-all(f16[16,1024,128]{2,1,0:T(8,128)(2,1)S(1)} %bitcast.24), channel_id=1, replica_groups={{0,1,2,3,4,5,6,7,8,9,10,11,12,13,14,15},{16,17,18,19,20,21,22,23,24,25,..., dimensions={0} | all-to-all | bytes 8388608 | tf_op jit(solution)/shard_map/all_to_all | solution.py:42
  85.7 0.6 convert_reduce_fusion
  86.3 0.7 fusion.11
  87.0 0.1 pad_maximum_fusion
  87.1 15.2 %all_to_all.27 = f16[4,264,128]{2,1,0:T(8,128)(2,1)S(1)} all-to-all(f16[4,264,128]{2,1,0:T(8,128)(2,1)S(1)} %pad_maximum_fusion), channel_id=1, replica_groups={{0,16,32,48},{8,24,40,56},{1,17,33,49},{9,25,41,57},{2,18,34,50},{10,26..., dimensions={0} | all-to-all | bytes 540672 | tf_op jit(solution)/shard_map/all_to_all | solution.py:42
  102.4 0.0 copy-start.5
  102.4 3.5 %collective-permute-start.3 = (f32[256,128]{1,0:T(8,128)S(1)}, f32[256,128]{1,0:T(8,128)S(1)}, u32[]{:S(2)}, u32[]{:S(2)}) collective-permute-start(f32[256,128]{1,0:T(8,128)S(1)} %fusion.9.fine_ref), channel_id=1, source_target_pairs={{0,0},{8,8},{16,64},{24,72},{32,128},{40,136},{48,192},{56,200},{6... | collective-permute-start | bytes 393224 | tf_op jit(solution)/shard_map/ppermute | solution.py:170
  105.9 0.2 squares.1
  106.1 21.3 %all_to_all.28.squares_ref = f32[32,1,128]{2,1,0:T(1,128)S(1)} all-to-all(f32[32,1,128]{2,1,0:T(1,128)S(1)} %squares.1), channel_id=1, replica_groups=mesh['tensor'=4,'dp'=8,'replica'=8] {'tensor','dp'}, dimensions={0} | all-to-all | bytes 32768 | tf_op jit(solution)/shard_map/all_to_all | solution.py:42
  127.4 0.1 pack.1
  127.5 12.6 %all_to_all.29 = f16[8,136,256]{2,1,0:T(8,128)(2,1)S(1)} all-to-all(f16[8,136,256]{2,1,0:T(8,128)(2,1)S(1)} %broadcast_in_dim.2), channel_id=1, replica_groups=mesh['tensor'=4,'dp'=8,'replica'=8] {'replica'}, dimensions={0} | all-to-all | bytes 1114112 | tf_op jit(solution)/shard_map/all_to_all | solution.py:42
  140.2 0.1 convert_element_type.20
  140.3 0.1 fusion.14
  140.3 0.1 slice_multiply_fusion
  140.5 2.2 %multiply_subtract_fusion = (f32[1024,256]{1,0:T(8,128)}, f32[1024,256]{1,0:T(8,128)}, f32[1024,256]{1,0:T(8,128)}) fusion(f32[1024,256]{1,0:T(8,128)S(1)} %copy-done.4, f32[8,128,256]{2,1,0:T(8,128)S(1)} %slice_multiply_fusion, f32[256]{0:T(256)S(1)} %rsqrt_minimum_fusion, f32[1024,256]{1,0:T(8,128)S(1)} %copy-done.5, f32[1024,256]{1,0:T(8,128)S(1)} %copy-done.6), kind=kLoop, calls=%fused_computation.15 | loop fusion | flops 4194304 | bytes 7341056 | tf_op jit(solution)/shard_map/sub | solution.py:184
  (24 shorter events, 0.2 us)
Async XLA Ops:
  0.6 25.3 %collective-permute-start.2 = (bf16[768,256]{1,0:T(8,128)(2,1)}, bf16[768,256]{1,0:T(8,128)(2,1)S(1)}, u32[]{:S(2)}, u32[]{:S(2)}) collective-permute-start(bf16[768,256]{1,0:T(8,128)(2,1)} %cotangent_ref.1), channel_id=1, source_target_pairs={{0,192},{64,128},{128,64},{192,0},{1,193},{65,129},{129,65},{193,1... | collective-permute-start | bytes 1179656 | tf_op jit(solution)/shard_map/ppermute | solution.py:51
  5.0 20.9 %collective-permute-start.1 = (bf16[768,256]{1,0:T(8,128)(2,1)}, bf16[768,256]{1,0:T(8,128)(2,1)S(1)}, u32[]{:S(2)}, u32[]{:S(2)}) collective-permute-start(bf16[768,256]{1,0:T(8,128)(2,1)} %cotangent_ref.1), channel_id=1, source_target_pairs={{0,128},{64,192},{128,0},{192,64},{1,129},{65,193},{129,1},{193,65... | collective-permute-start | bytes 1179656 | tf_op jit(solution)/shard_map/ppermute | solution.py:51
  6.8 19.2 %collective-permute-start = (bf16[768,256]{1,0:T(8,128)(2,1)}, bf16[768,256]{1,0:T(8,128)(2,1)S(1)}, u32[]{:S(2)}, u32[]{:S(2)}) collective-permute-start(bf16[768,256]{1,0:T(8,128)(2,1)} %cotangent_ref.1), channel_id=1, source_target_pairs={{0,64},{64,0},{128,192},{192,128},{1,65},{65,1},{129,193},{193,129... | collective-permute-start | bytes 1179656 | tf_op jit(solution)/shard_map/ppermute | solution.py:51
  6.8 1.9 %copy-start = (bf16[768,2048]{1,0:T(8,128)(2,1)S(1)}, bf16[768,2048]{1,0:T(8,128)(2,1)}, u32[]{:S(2)}) copy-start(bf16[768,2048]{1,0:T(8,128)(2,1)} %features_ref.1) | copy-start | bytes 9437188
  8.7 1.0 copy-start.2
  9.7 16.3 %copy-start.1 = (bf16[768,2048]{1,0:T(8,128)(2,1)S(1)}, bf16[768,2048]{1,0:T(8,128)(2,1)}, u32[]{:S(2)}) copy-start(bf16[768,2048]{1,0:T(8,128)(2,1)} %features_ref.1) | copy-start | bytes 9437188
  9.7 16.3 %copy-start.3 = (bf16[768,256]{1,0:T(8,128)(2,1)S(1)}, bf16[768,256]{1,0:T(8,128)(2,1)}, u32[]{:S(2)}) copy-start(bf16[768,256]{1,0:T(8,128)(2,1)} %cotangent_ref.1) | copy-start | bytes 1179652
  102.4 38.1 %copy-start.4 = (f32[1024,256]{1,0:T(8,128)S(1)}, f32[1024,256]{1,0:T(8,128)}, u32[]{:S(2)}) copy-start(f32[1024,256]{1,0:T(8,128)} %param.7) | copy-start | bytes 3145732
  102.4 38.1 %copy-start.5 = (f32[1024,256]{1,0:T(8,128)S(1)}, f32[1024,256]{1,0:T(8,128)}, u32[]{:S(2)}) copy-start(f32[1024,256]{1,0:T(8,128)} %param.8) | copy-start | bytes 3145732
  102.4 38.1 %copy-start.6 = (f32[1024,256]{1,0:T(8,128)S(1)}, f32[1024,256]{1,0:T(8,128)}, u32[]{:S(2)}) copy-start(f32[1024,256]{1,0:T(8,128)} %param.9) | copy-start | bytes 3145732
  102.4 25.0 %collective-permute-start.3 = (f32[256,128]{1,0:T(8,128)S(1)}, f32[256,128]{1,0:T(8,128)S(1)}, u32[]{:S(2)}, u32[]{:S(2)}) collective-permute-start(f32[256,128]{1,0:T(8,128)S(1)} %fusion.9.fine_ref), channel_id=1, source_target_pairs={{0,0},{8,8},{16,64},{24,72},{32,128},{40,136},{48,192},{56,200},{6... | collective-permute-start | bytes 393224 | tf_op jit(solution)/shard_map/ppermute | solution.py:170

commit v4 on v3

--- a/solution.py
+++ b/solution.py
@@ -21,7 +21,6 @@
 weight_decay = 0.1
 
 EVERY = ("tensor", "dp", "replica")
-SUMMED = ("dp", "replica")
 LINK = jnp.float16
 LINK_TOP = 60000.0
 LEAST = 1e-30
@@ -70,7 +69,8 @@
     )(features, cotangent)
 
 
-def scale_kernel(terms, tops_ref, down_ref, exponent_ref):
+def ready_kernel(terms, tops_ref, *refs):
+    *blocks, columns_ref, down_ref, exponent_ref = refs
     tops = jnp.max(tops_ref[...], axis=0)
     lane = lax.broadcasted_iota(jnp.int32, tops.shape, 1)
     feat_top = jnp.max(jnp.where(lane == 0, tops, 0.0))
@@ -79,19 +79,25 @@
     exponent = jnp.ceil(jnp.log2(bound * (1.0 / LINK_TOP)))
     down_ref[...] = jnp.exp2(-exponent)[:1, :1]
     exponent_ref[...] = exponent[:1, :1]
+    cols = blocks[0].shape[1]
+    me = lax.axis_index("tensor")
+    for j, block in enumerate(blocks):
+        place = pl.multiple_of((me ^ j) * cols, cols)
+        columns_ref[:, pl.ds(place, cols)] = block[...]
 
 
-def scale_for(tops, terms):
+def ready(tops, blocks, terms):
     one = jax.ShapeDtypeStruct((1, 1), F32)
-    down, exponent = pl.pallas_call(
-        functools.partial(scale_kernel, terms),
-        in_specs=[WHOLE],
-        out_specs=[WHOLE] * 2,
-        out_shape=[one, one],
+    tokens, cols = blocks[0].shape
+    columns, down, exponent = pl.pallas_call(
+        functools.partial(ready_kernel, terms),
+        in_specs=[WHOLE] * (1 + len(blocks)),
+        out_specs=[WHOLE] * 3,
+        out_shape=[jax.ShapeDtypeStruct((tokens, cols * len(blocks)), blocks[0].dtype), one, one],
         compiler_params=SMALL,
-        name="scale",
-    )(tops)
-    return down.reshape(()), exponent.reshape(())
+        name="ready",
+    )(tops, *blocks)
+    return columns, down.reshape(()), exponent.reshape(())
 
 
 def squares_kernel(fine_ref, out_ref):
@@ -119,7 +125,8 @@
     high = jnp.floor(level * 2048.0) * (1.0 / 2048.0)
     low = (level - high) * 2048.0
     row = lax.broadcasted_iota(jnp.int32, (TOLD, cols), 0)
-    out_ref[:part] = moved_ref[...].T * scale
+    block = moved_ref[...].T * scale
+    out_ref[:part] = block * jnp.abs(block) * (1.0 / LINK_TOP)
     out_ref[part:] = jnp.where(row == 0, exponent, jnp.where(row == 1, high, low))
 
 
@@ -143,37 +150,29 @@
     halves = dp // tensor
     part = rows // halves // replica
     run = halves * replica
-    runs = [list(range(i * run, (i + 1) * run)) for i in range(tensor)]
-    blocks_of_runs = [[t * dp * replica + i for t in range(tensor) for i in r] for r in runs]
+    runs = [[t * dp * replica + i * run + s for s in range(run) for t in range(tensor)] for i in range(tensor)]
     apart = [[i * halves + h for i in range(tensor)] for h in range(halves)]
 
-    columns = [cotangent] + [partner(cotangent, j) for j in range(1, tensor)]
-    columns = jnp.concatenate(columns, axis=1)
-
-    tops = swap(tops_of(features, cotangent, tensor * run), EVERY, blocks_of_runs)
-    down, exponent = scale_for(tops, tokens * run)
-
+    blocks = [cotangent] + [partner(cotangent, j) for j in range(1, tensor)]
+    tops = swap(tops_of(features, cotangent, tensor * run), EVERY, runs)
+    columns, down, exponent = ready(tops, blocks, tokens * run)
     partial = (contract_tokens(columns, features) * down).astype(LINK)
     partial = partial.reshape(total_cols, run, part).transpose(1, 0, 2)
-    mine = jnp.sum(swap(partial, SUMMED, runs).astype(F32), axis=0).reshape(tensor, cols, part)
+    got = swap(partial.reshape(run * tensor, cols, part), EVERY, runs)
+    mine = jnp.sum(got.reshape(run, tensor, cols, part).astype(F32), axis=0)
     note = exponent + 0.0 * mine[:, :TOLD]
     message = jnp.concatenate([mine, note], axis=1).astype(LINK)
     got = swap(message, "dp", apart).astype(F32)
     fine = jnp.sum(got[:, :cols] * jnp.exp2(got[:, cols : cols + 1]), axis=0)
 
-    to_owner = [
-        (t * dp + j * halves + h, (t ^ j) * dp + t * halves + h)
-        for t in range(tensor)
-        for j in range(tensor)
-        for h in range(halves)
-    ]
-    moved = lax.ppermute(fine, ("tensor", "dp"), to_owner)
     squares = swap(squares_of(fine, tensor * dp), ("tensor", "dp"))
-    told = spread(pack(moved, squares).astype(LINK), "replica", replica).astype(F32)
+    told = spread(pack(fine, squares).astype(LINK), "replica", replica).astype(F32)
     factors = jnp.exp2(told[:, part : part + 1])
     halfway = told[:, part + 1 : part + 2] + told[:, part + 2 : part + 3] * (1.0 / 2048.0)
     square_sum = jnp.sum(halfway * factors * factors, axis=0) * LINK_TOP**2
-    grad = (told[:, :part] * factors).reshape(replica * part, cols)
+    level = told[:, :part]
+    size = jnp.sqrt(jnp.abs(level)) * (factors * LINK_TOP**0.5)
+    grad = jnp.where(level < 0.0, -size, size).reshape(replica * part, cols)
 
     mean_square = square_sum / (D * total_cols)
     clip = jnp.minimum(1.0, clip_level / jnp.sqrt(mean_square + norm_eps))

time: 143 us -> 140 us (0.979)
  starting transfers between devices: 9.67 us -> 6.47 us
    ppermute x1 -> x0, starting transfers between devices: 3.49 us -> none  [body(): moved = lax.ppermute(fine, ('tensor', 'dp'), to_owner)]
    unnamed x15 -> x13, local copies, waits for them, and re-layouts: 2.91 us -> 2.91 us
  transfers between devices with their start and end apart: 4 -> 3, of which waited for: 0 -> 0; matrix products, arithmetic and copies ran while one was open for 0% -> 0% of each run, Pallas kernels for 1% -> 0%
where the time goes in v4:
time: 140 us
  blocking collectives  118 us (84%)
  starting transfers between devices  6.47 us (5%)
  matrix products  4.38 us (3%)
  other arithmetic  4.35 us (3%)
  local copies, waits for them, and re-layouts  3.96 us (3%)
    all_to_all x5, blocking collectives, swap(): lax.all_to_all(x, axis, split_axis=0, concat_axis=0, axis_index_groups=gr...  118 us
    ppermute x3, starting transfers between devices, partner(): return lax.ppermute(x, 'tensor', [(i, i ^ bit) for i in range(count)])  6.47 us
    dot_general x1, matrix products, contract_tokens(): lax.dot_general(left, right, (((0,), (0,)), ((), ())), preferred_element_...  4.38 us
    unnamed x13, local copies, waits for them, and re-layouts  2.91 us
  transfers between devices with their start and end apart: 3, of which 0 were waited for; matrix products, arithmetic and copies ran while one was open for 0% of the time, Pallas kernels for 0%

profile of v4, /device:TPU:1, one launch (start us, length us, event | category | flops | bytes accessed | tf_op | source)
XLA Modules:
  0.0 139.5 jit_solution(17406377583559520691)
XLA Ops:
  0.6 3.8 %collective-permute-start.1 = (bf16[768,256]{1,0:T(8,128)(2,1)}, bf16[768,256]{1,0:T(8,128)(2,1)S(1)}, u32[]{:S(2)}, u32[]{:S(2)}) collective-permute-start(bf16[768,256]{1,0:T(8,128)(2,1)} %refs_0_.1), channel_id=1, source_target_pairs={{0,128},{64,192},{128,0},{192,64},{1,129},{65,193},{129,1},{193,65... | collective-permute-start | bytes 1179656 | tf_op jit(solution)/shard_map/ppermute | solution.py:50
  4.5 1.0 collective-permute-start
  5.4 1.7 %collective-permute-start.2 = (bf16[768,256]{1,0:T(8,128)(2,1)}, bf16[768,256]{1,0:T(8,128)(2,1)S(1)}, u32[]{:S(2)}, u32[]{:S(2)}) collective-permute-start(bf16[768,256]{1,0:T(8,128)(2,1)} %refs_0_.1), channel_id=1, source_target_pairs={{0,192},{64,128},{128,64},{192,0},{1,193},{65,129},{129,65},{193,1... | collective-permute-start | bytes 1179656 | tf_op jit(solution)/shard_map/ppermute | solution.py:50
  7.1 1.9 %copy-done = bf16[768,2048]{1,0:T(8,128)(2,1)S(1)} copy-done((bf16[768,2048]{1,0:T(8,128)(2,1)S(1)}, bf16[768,2048]{1,0:T(8,128)(2,1)}, u32[]{:S(2)}) %copy-start) | copy-done | bytes 3145752
  9.0 1.0 copy-done.2
  10.0 0.3 tops.1
  10.3 15.5 %all_to_all.25.tops_ref = f32[64,1,128]{2,1,0:T(1,128)S(1)} all-to-all(f32[64,1,128]{2,1,0:T(1,128)S(1)} %tops.1), channel_id=1, replica_groups={{0,64,128,192,1,65,129,193,2,66,130,194,3,67,131,195,4,68,132,196,5,69,..., dimensions={0} | all-to-all | bytes 65536 | tf_op jit(solution)/shard_map/all_to_all | solution.py:41
  25.7 0.8 ready.1
  26.5 4.4 %fusion = f16[128,16,8,128]{3,2,1,0:T(8,128)(2,1)S(1)} fusion(f32[]{:T(128)} %bitcast, bf16[768,1024]{1,0:T(8,128)(2,1)S(1)} %get-tuple-element.6, bf16[768,2048]{1,0:T(8,128)(2,1)S(1)} %copy-done.1), kind=kOutput, calls=%fused_computation.3 | convolution fusion | flops 3225419776 | bytes 8912900 | tf_op jit(solution)/shard_map/dot_general | solution.py:35
  30.9 1.0 copy.14
  31.9 56.8 %all_to_all.26 = f16[64,256,128]{2,1,0:T(8,128)(2,1)S(1)} all-to-all(f16[64,256,128]{2,1,0:T(8,128)(2,1)S(1)} %bitcast.26), channel_id=1, replica_groups={{0,64,128,192,1,65,129,193,2,66,130,194,3,67,131,195,4,68,132,196,5,69,..., dimensions={0} | all-to-all | bytes 8388608 | tf_op jit(solution)/shard_map/all_to_all | solution.py:41
  88.7 0.7 convert_reduce_fusion
  89.5 0.7 fusion.4
  90.1 0.1 pad_maximum_fusion
  90.2 15.7 %all_to_all.27 = f16[4,264,128]{2,1,0:T(8,128)(2,1)S(1)} all-to-all(f16[4,264,128]{2,1,0:T(8,128)(2,1)S(1)} %pad_maximum_fusion), channel_id=1, replica_groups={{0,16,32,48},{8,24,40,56},{1,17,33,49},{9,25,41,57},{2,18,34,50},{10,26..., dimensions={0} | all-to-all | bytes 540672 | tf_op jit(solution)/shard_map/all_to_all | solution.py:41
  106.1 0.0 copy-start.5
  106.1 0.2 squares.1
  106.3 17.4 %all_to_all.28.squares_ref = f32[32,1,128]{2,1,0:T(1,128)S(1)} all-to-all(f32[32,1,128]{2,1,0:T(1,128)S(1)} %squares.1), channel_id=1, replica_groups=mesh['tensor'=4,'dp'=8,'replica'=8] {'tensor','dp'}, dimensions={0} | all-to-all | bytes 32768 | tf_op jit(solution)/shard_map/all_to_all | solution.py:41
  123.7 0.1 pack.1
  123.8 12.9 %all_to_all.29 = f16[8,136,256]{2,1,0:T(8,128)(2,1)S(1)} all-to-all(f16[8,136,256]{2,1,0:T(8,128)(2,1)S(1)} %broadcast_in_dim.2), channel_id=1, replica_groups=mesh['tensor'=4,'dp'=8,'replica'=8] {'replica'}, dimensions={0} | all-to-all | bytes 1114112 | tf_op jit(solution)/shard_map/all_to_all | solution.py:41
  136.7 0.1 convert_element_type.24
  136.8 0.1 fusion.7
  136.9 0.4 negate_select_fusion
  137.3 2.2 %multiply_subtract_fusion = (f32[1024,256]{1,0:T(8,128)}, f32[1024,256]{1,0:T(8,128)}, f32[1024,256]{1,0:T(8,128)}) fusion(f32[1024,256]{1,0:T(8,128)S(1)} %copy-done.3, f32[8,128,256]{2,1,0:T(8,128)S(1)} %negate_select_fusion, f32[256]{0:T(256)S(1)} %rsqrt_minimum_fusion, f32[1024,256]{1,0:T(8,128)S(1)} %copy-done.4, f32[1024,256]{1,0:T(8,128)S(1)} %copy-done.5), kind=kLoop, calls=%fused_computation.8 | loop fusion | flops 4194304 | bytes 7341056 | tf_op jit(solution)/shard_map/sub | solution.py:183
  (20 shorter events, 0.2 us)
Async XLA Ops:
  0.6 25.1 %collective-permute-start.1 = (bf16[768,256]{1,0:T(8,128)(2,1)}, bf16[768,256]{1,0:T(8,128)(2,1)S(1)}, u32[]{:S(2)}, u32[]{:S(2)}) collective-permute-start(bf16[768,256]{1,0:T(8,128)(2,1)} %refs_0_.1), channel_id=1, source_target_pairs={{0,128},{64,192},{128,0},{192,64},{1,129},{65,193},{129,1},{193,65... | collective-permute-start | bytes 1179656 | tf_op jit(solution)/shard_map/ppermute | solution.py:50
  4.5 21.3 %collective-permute-start = (bf16[768,256]{1,0:T(8,128)(2,1)}, bf16[768,256]{1,0:T(8,128)(2,1)S(1)}, u32[]{:S(2)}, u32[]{:S(2)}) collective-permute-start(bf16[768,256]{1,0:T(8,128)(2,1)} %refs_0_.1), channel_id=1, source_target_pairs={{0,64},{64,0},{128,192},{192,128},{1,65},{65,1},{129,193},{193,129... | collective-permute-start | bytes 1179656 | tf_op jit(solution)/shard_map/ppermute | solution.py:50
  5.4 20.3 %collective-permute-start.2 = (bf16[768,256]{1,0:T(8,128)(2,1)}, bf16[768,256]{1,0:T(8,128)(2,1)S(1)}, u32[]{:S(2)}, u32[]{:S(2)}) collective-permute-start(bf16[768,256]{1,0:T(8,128)(2,1)} %refs_0_.1), channel_id=1, source_target_pairs={{0,192},{64,128},{128,64},{192,0},{1,193},{65,129},{129,65},{193,1... | collective-permute-start | bytes 1179656 | tf_op jit(solution)/shard_map/ppermute | solution.py:50
  7.1 1.9 %copy-start = (bf16[768,2048]{1,0:T(8,128)(2,1)S(1)}, bf16[768,2048]{1,0:T(8,128)(2,1)}, u32[]{:S(2)}) copy-start(bf16[768,2048]{1,0:T(8,128)(2,1)} %features_ref.1) | copy-start | bytes 9437188
  9.0 1.0 copy-start.2
  10.0 16.5 %copy-start.1 = (bf16[768,2048]{1,0:T(8,128)(2,1)S(1)}, bf16[768,2048]{1,0:T(8,128)(2,1)}, u32[]{:S(2)}) copy-start(bf16[768,2048]{1,0:T(8,128)(2,1)} %features_ref.1) | copy-start | bytes 9437188
  106.1 31.3 %copy-start.3 = (f32[1024,256]{1,0:T(8,128)S(1)}, f32[1024,256]{1,0:T(8,128)}, u32[]{:S(2)}) copy-start(f32[1024,256]{1,0:T(8,128)} %param.7) | copy-start | bytes 3145732
  106.1 31.2 %copy-start.4 = (f32[1024,256]{1,0:T(8,128)S(1)}, f32[1024,256]{1,0:T(8,128)}, u32[]{:S(2)}) copy-start(f32[1024,256]{1,0:T(8,128)} %param.8) | copy-start | bytes 3145732
  106.1 31.2 %copy-start.5 = (f32[1024,256]{1,0:T(8,128)S(1)}, f32[1024,256]{1,0:T(8,128)}, u32[]{:S(2)}) copy-start(f32[1024,256]{1,0:T(8,128)} %param.9) | copy-start | bytes 3145732

commit v5 on v4

--- a/solution.py
+++ b/solution.py
@@ -50,53 +50,55 @@
     return lax.ppermute(x, "tensor", [(i, i ^ bit) for i in range(count)])
 
 
-def tops_kernel(features_ref, cotangent_ref, out_ref):
-    feat_top = jnp.max(jnp.max(jnp.abs(features_ref[...]).reshape(-1, 16, features_ref.shape[1]), axis=0).astype(F32))
-    cot_top = jnp.max(jnp.max(jnp.abs(cotangent_ref[...]).reshape(-1, 16, cotangent_ref.shape[1]), axis=0).astype(F32))
-    lane = lax.broadcasted_iota(jnp.int32, out_ref.shape, 2)
-    out_ref[...] = jnp.where(lane == 0, feat_top, cot_top)
-
-
-def tops_of(features, cotangent, count):
-    return pl.pallas_call(
-        tops_kernel,
-        in_specs=[WHOLE] * 2,
-        out_specs=WHOLE,
-        out_shape=jax.ShapeDtypeStruct((count, 1, LANES), F32),
-        compiler_params=pltpu.CompilerParams(vmem_limit_bytes=16 * 2**20),
-        cost_estimate=pl.CostEstimate(flops=2 * features.size, bytes_accessed=2 * features.size, transcendentals=0),
-        name="tops",
-    )(features, cotangent)
-
-
-def ready_kernel(terms, tops_ref, *refs):
+def top_of(ref):
+    return jnp.max(jnp.max(jnp.abs(ref[...]).reshape(-1, 16, ref.shape[1]), axis=0).astype(F32))
+
+
+def own_kernel(features_ref, own_ref, copy_ref, top_ref):
+    copy_ref[...] = own_ref[...]
+    top_ref[...] = jnp.full(top_ref.shape, top_of(features_ref))
+
+
+def columns_kernel(top_ref, *refs):
     *blocks, columns_ref, down_ref, exponent_ref = refs
-    tops = jnp.max(tops_ref[...], axis=0)
-    lane = lax.broadcasted_iota(jnp.int32, tops.shape, 1)
-    feat_top = jnp.max(jnp.where(lane == 0, tops, 0.0))
-    cot_top = jnp.max(jnp.where(lane == 0, 0.0, tops))
-    bound = jnp.maximum(jnp.full((8, LANES), feat_top) * cot_top * terms, LEAST)
-    exponent = jnp.ceil(jnp.log2(bound * (1.0 / LINK_TOP)))
-    down_ref[...] = jnp.exp2(-exponent)[:1, :1]
-    exponent_ref[...] = exponent[:1, :1]
-    cols = blocks[0].shape[1]
+    tokens, cols = blocks[0].shape
     me = lax.axis_index("tensor")
     for j, block in enumerate(blocks):
         place = pl.multiple_of((me ^ j) * cols, cols)
         columns_ref[:, pl.ds(place, cols)] = block[...]
-
-
-def ready(tops, blocks, terms):
+    cot_top = functools.reduce(jnp.maximum, [top_of(block) for block in blocks])
+    bound = jnp.maximum(top_ref[...] * cot_top * tokens, LEAST)
+    exponent = jnp.ceil(jnp.log2(bound * (1.0 / LINK_TOP)))
+    down_ref[...] = jnp.exp2(-exponent)[:1, :1]
+    exponent_ref[...] = exponent[:1, :1]
+
+
+def own_part(features, own):
+    return pl.pallas_call(
+        own_kernel,
+        in_specs=[WHOLE] * 2,
+        out_specs=[WHOLE] * 2,
+        out_shape=[
+            jax.ShapeDtypeStruct(own.shape, own.dtype),
+            jax.ShapeDtypeStruct((8, LANES), F32),
+        ],
+        compiler_params=pltpu.CompilerParams(vmem_limit_bytes=16 * 2**20),
+        cost_estimate=pl.CostEstimate(flops=2 * features.size, bytes_accessed=2 * features.size, transcendentals=0),
+        name="own",
+    )(features, own)
+
+
+def whole_columns(top, blocks):
     one = jax.ShapeDtypeStruct((1, 1), F32)
     tokens, cols = blocks[0].shape
     columns, down, exponent = pl.pallas_call(
-        functools.partial(ready_kernel, terms),
+        columns_kernel,
         in_specs=[WHOLE] * (1 + len(blocks)),
         out_specs=[WHOLE] * 3,
         out_shape=[jax.ShapeDtypeStruct((tokens, cols * len(blocks)), blocks[0].dtype), one, one],
         compiler_params=SMALL,
-        name="ready",
-    )(tops, *blocks)
+        name="columns",
+    )(top, *blocks)
     return columns, down.reshape(()), exponent.reshape(())
 
 
@@ -153,15 +155,24 @@
     runs = [[t * dp * replica + i * run + s for s in range(run) for t in range(tensor)] for i in range(tensor)]
     apart = [[i * halves + h for i in range(tensor)] for h in range(halves)]
 
-    blocks = [cotangent] + [partner(cotangent, j) for j in range(1, tensor)]
-    tops = swap(tops_of(features, cotangent, tensor * run), EVERY, runs)
-    columns, down, exponent = ready(tops, blocks, tokens * run)
+    near, away = partner(cotangent, 1), partner(cotangent, 2)
+    own, top = own_part(features, cotangent)
+    away, top = lax.optimization_barrier((away, top))
+    columns, down, exponent = whole_columns(top, [own, near, away, partner(away, 1)])
+
     partial = (contract_tokens(columns, features) * down).astype(LINK)
-    partial = partial.reshape(total_cols, run, part).transpose(1, 0, 2)
-    got = swap(partial.reshape(run * tensor, cols, part), EVERY, runs)
-    mine = jnp.sum(got.reshape(run, tensor, cols, part).astype(F32), axis=0)
-    note = exponent + 0.0 * mine[:, :TOLD]
-    message = jnp.concatenate([mine, note], axis=1).astype(LINK)
+    partial = partial.reshape(total_cols // TOLD, TOLD, run, part).transpose(2, 0, 1, 3)
+    partial = partial.reshape(run, tensor, cols // TOLD, TOLD, part)
+    note = jnp.broadcast_to(exponent.astype(LINK), (run, tensor, 1, TOLD, part))
+    message = jnp.concatenate([partial, note], axis=2)
+    got = swap(message.reshape(run * tensor, cols + TOLD, part), EVERY, runs)
+    got = got.reshape(run, tensor, cols + TOLD, part)
+    factors = jnp.exp2(got[:, :, cols : cols + 1].astype(F32))
+    mine = jnp.sum(got[:, :, :cols].astype(F32) * factors, axis=0)
+    exponent = jnp.ceil(jnp.log2(jnp.sum(factors, axis=0)))
+
+    note = jnp.broadcast_to(exponent, (tensor, TOLD, part))
+    message = jnp.concatenate([mine * jnp.exp2(-exponent), note], axis=1).astype(LINK)
     got = swap(message, "dp", apart).astype(F32)
     fine = jnp.sum(got[:, :cols] * jnp.exp2(got[:, cols : cols + 1]), axis=0)
 

time: 140 us -> 136 us (0.971)
  blocking collectives: 118 us -> 107 us
  waiting for transfers between devices: 0.01 us -> 5.31 us
    all_to_all x5 -> x4, blocking collectives: 118 us -> 107 us  [swap(): lax.all_to_all(x, axis, split_axis=0, concat_axis=0, axis_index_groups=gr...]
    ppermute x3, waiting for transfers between devices: 0.01 us -> 5.31 us  [partner(): return lax.ppermute(x, 'tensor', [(i, i ^ bit) for i in range(count)])]
  transfers between devices with their start and end apart: 3 -> 3, of which waited for: 0 -> 2; matrix products, arithmetic and copies ran while one was open for 0% -> 0% of each run, Pallas kernels for 0% -> 0%
where the time goes in v5:
time: 136 us
  blocking collectives  107 us (79%)
  starting transfers between devices  6.97 us (5%)
  waiting for transfers between devices  5.31 us (4%)
  local copies, waits for them, and re-layouts  4.86 us (4%)
  matrix products  4.38 us (3%)
  other arithmetic  3.92 us (3%)
  Pallas kernels  1.56 us (1%)
  between operations  1.49 us (1%)
    all_to_all x4, blocking collectives, swap(): lax.all_to_all(x, axis, split_axis=0, concat_axis=0, axis_index_groups=gr...  107 us
    ppermute x3, starting transfers between devices, partner(): return lax.ppermute(x, 'tensor', [(i, i ^ bit) for i in range(count)])  6.97 us
    ppermute x3, waiting for transfers between devices, partner(): return lax.ppermute(x, 'tensor', [(i, i ^ bit) for i in range(count)])  5.31 us
    dot_general x1, matrix products, contract_tokens(): lax.dot_general(left, right, (((0,), (0,)), ((), ())), preferred_element_...  4.38 us
    unnamed x13, local copies, waits for them, and re-layouts  2.91 us
  transfers between devices with their start and end apart: 3, of which 2 were waited for; matrix products, arithmetic and copies ran while one was open for 0% of the time, Pallas kernels for 0%

profile of v5, /device:TPU:1, one launch (start us, length us, event | category | flops | bytes accessed | tf_op | source)
XLA Modules:
  0.0 135.6 jit_solution(1763651580270426373)
XLA Ops:
  0.6 3.8 %collective-permute-start = (bf16[768,256]{1,0:T(8,128)(2,1)}, bf16[768,256]{1,0:T(8,128)(2,1)S(1)}, u32[]{:S(2)}, u32[]{:S(2)}) collective-permute-start(bf16[768,256]{1,0:T(8,128)(2,1)} %own_ref.1), channel_id=1, source_target_pairs={{0,128},{64,192},{128,0},{192,64},{1,129},{65,193},{129,1},{193,65... | collective-permute-start | bytes 1179656 | tf_op jit(solution)/shard_map/ppermute | solution.py:50
  4.5 1.0 collective-permute-start.1
  5.4 1.9 %copy-done = bf16[768,2048]{1,0:T(8,128)(2,1)S(1)} copy-done((bf16[768,2048]{1,0:T(8,128)(2,1)S(1)}, bf16[768,2048]{1,0:T(8,128)(2,1)}, u32[]{:S(2)}) %copy-start) | copy-done | bytes 3145752
  7.3 1.0 copy-done.2
  8.3 0.3 own.1
  8.6 4.0 %collective-permute-done.refs_2_ = bf16[768,256]{1,0:T(8,128)(2,1)S(1)} collective-permute-done((bf16[768,256]{1,0:T(8,128)(2,1)}, bf16[768,256]{1,0:T(8,128)(2,1)S(1)}, u32[]{:S(2)}, u32[]{:S(2)}) %collective-permute-start) | collective-permute-done | bytes 393248 | tf_op jit(solution)/shard_map/ppermute | solution.py:50
  12.6 2.2 %collective-permute-start.2 = (bf16[768,256]{1,0:T(8,128)(2,1)S(1)}, bf16[768,256]{1,0:T(8,128)(2,1)S(1)}, u32[]{:S(2)}, u32[]{:S(2)}) collective-permute-start(bf16[768,256]{1,0:T(8,128)(2,1)S(1)} %collective-permute-done.refs_2_), channel_id=1, source_target_pairs={{0,64},{64,0},{128,192},{192,128},{1,65},{65,1},{129,193},{193,129... | collective-permute-start | bytes 1179656 | tf_op jit(solution)/shard_map/ppermute | solution.py:50
  14.7 1.3 collective-permute-done.2.refs_3_
  16.1 1.0 columns.1
  17.8 4.4 %fusion = f16[16,128,8,128]{3,2,0,1:T(8,128)(2,1)S(1)} fusion(f32[]{:T(128)} %bitcast, bf16[768,1024]{1,0:T(8,128)(2,1)S(1)} %get-tuple-element.14, bf16[768,2048]{1,0:T(8,128)(2,1)S(1)} %copy-done.1), kind=kOutput, calls=%fused_computation.2 | convolution fusion | flops 3225419776 | bytes 8912900 | tf_op jit(solution)/shard_map/dot_general | solution.py:35
  22.2 1.0 copy.9
  23.2 0.9 concatenate.7
  24.1 62.6 %all_to_all.20 = f16[64,264,128]{2,1,0:T(8,128)(2,1)S(1)} all-to-all(f16[64,264,128]{2,1,0:T(8,128)(2,1)S(1)} %bitcast.24), channel_id=1, replica_groups={{0,64,128,192,1,65,129,193,2,66,130,194,3,67,131,195,4,68,132,196,5,69,..., dimensions={0} | all-to-all | bytes 8650752 | tf_op jit(solution)/shard_map/all_to_all | solution.py:41
  86.7 0.1 fusion.11
  86.8 0.9 multiply_reduce_fusion
  87.7 0.1 pad_maximum_fusion
  87.9 17.0 %all_to_all.21 = f16[4,264,128]{2,1,0:T(8,128)(2,1)S(1)} all-to-all(f16[4,264,128]{2,1,0:T(8,128)(2,1)S(1)} %pad_maximum_fusion), channel_id=1, replica_groups={{0,16,32,48},{8,24,40,56},{1,17,33,49},{9,25,41,57},{2,18,34,50},{10,26..., dimensions={0} | all-to-all | bytes 540672 | tf_op jit(solution)/shard_map/all_to_all | solution.py:41
  105.0 0.2 squares.1
  105.2 15.3 %all_to_all.22.squares_ref = f32[32,1,128]{2,1,0:T(1,128)S(1)} all-to-all(f32[32,1,128]{2,1,0:T(1,128)S(1)} %squares.1), channel_id=1, replica_groups=mesh['tensor'=4,'dp'=8,'replica'=8] {'tensor','dp'}, dimensions={0} | all-to-all | bytes 32768 | tf_op jit(solution)/shard_map/all_to_all | solution.py:41
  120.5 0.1 pack.1
  120.6 12.2 %all_to_all.23 = f16[8,136,256]{2,1,0:T(8,128)(2,1)S(1)} all-to-all(f16[8,136,256]{2,1,0:T(8,128)(2,1)S(1)} %broadcast_in_dim.5), channel_id=1, replica_groups=mesh['tensor'=4,'dp'=8,'replica'=8] {'replica'}, dimensions={0} | all-to-all | bytes 1114112 | tf_op jit(solution)/shard_map/all_to_all | solution.py:41
  132.8 0.1 convert_element_type.32
  133.0 0.4 negate_select_fusion
  133.4 2.2 %multiply_subtract_fusion = (f32[1024,256]{1,0:T(8,128)}, f32[1024,256]{1,0:T(8,128)}, f32[1024,256]{1,0:T(8,128)}) fusion(f32[1024,256]{1,0:T(8,128)S(1)} %copy-done.3, f32[8,128,256]{2,1,0:T(8,128)S(1)} %negate_select_fusion, f32[256]{0:T(256)S(1)} %rsqrt_minimum_fusion, f32[1024,256]{1,0:T(8,128)S(1)} %copy-done.4, f32[1024,256]{1,0:T(8,128)S(1)} %copy-done.5), kind=kLoop, calls=%fused_computation.7 | loop fusion | flops 4194304 | bytes 7341056 | tf_op jit(solution)/shard_map/sub | solution.py:194
  (22 shorter events, 0.3 us)
Async XLA Ops:
  0.6 11.9 %collective-permute-start = (bf16[768,256]{1,0:T(8,128)(2,1)}, bf16[768,256]{1,0:T(8,128)(2,1)S(1)}, u32[]{:S(2)}, u32[]{:S(2)}) collective-permute-start(bf16[768,256]{1,0:T(8,128)(2,1)} %own_ref.1), channel_id=1, source_target_pairs={{0,128},{64,192},{128,0},{192,64},{1,129},{65,193},{129,1},{193,65... | collective-permute-start | bytes 1179656 | tf_op jit(solution)/shard_map/ppermute | solution.py:50
  4.5 10.3 %collective-permute-start.1 = (bf16[768,256]{1,0:T(8,128)(2,1)}, bf16[768,256]{1,0:T(8,128)(2,1)S(1)}, u32[]{:S(2)}, u32[]{:S(2)}) collective-permute-start(bf16[768,256]{1,0:T(8,128)(2,1)} %own_ref.1), channel_id=1, source_target_pairs={{0,64},{64,0},{128,192},{192,128},{1,65},{65,1},{129,193},{193,129... | collective-permute-start | bytes 1179656 | tf_op jit(solution)/shard_map/ppermute | solution.py:50
  5.4 1.9 %copy-start = (bf16[768,2048]{1,0:T(8,128)(2,1)S(1)}, bf16[768,2048]{1,0:T(8,128)(2,1)}, u32[]{:S(2)}) copy-start(bf16[768,2048]{1,0:T(8,128)(2,1)} %features_ref.1) | copy-start | bytes 9437188
  7.3 1.0 copy-start.2
  8.3 9.5 %copy-start.1 = (bf16[768,2048]{1,0:T(8,128)(2,1)S(1)}, bf16[768,2048]{1,0:T(8,128)(2,1)}, u32[]{:S(2)}) copy-start(bf16[768,2048]{1,0:T(8,128)(2,1)} %features_ref.1) | copy-start | bytes 9437188
  12.6 3.5 %collective-permute-start.2 = (bf16[768,256]{1,0:T(8,128)(2,1)S(1)}, bf16[768,256]{1,0:T(8,128)(2,1)S(1)}, u32[]{:S(2)}, u32[]{:S(2)}) collective-permute-start(bf16[768,256]{1,0:T(8,128)(2,1)S(1)} %collective-permute-done.refs_2_), channel_id=1, source_target_pairs={{0,64},{64,0},{128,192},{192,128},{1,65},{65,1},{129,193},{193,129... | collective-permute-start | bytes 1179656 | tf_op jit(solution)/shard_map/ppermute | solution.py:50
  87.8 45.6 %copy-start.3 = (f32[1024,256]{1,0:T(8,128)S(1)}, f32[1024,256]{1,0:T(8,128)}, u32[]{:S(2)}) copy-start(f32[1024,256]{1,0:T(8,128)} %param.7) | copy-start | bytes 3145732
  87.8 45.6 %copy-start.4 = (f32[1024,256]{1,0:T(8,128)S(1)}, f32[1024,256]{1,0:T(8,128)}, u32[]{:S(2)}) copy-start(f32[1024,256]{1,0:T(8,128)} %param.8) | copy-start | bytes 3145732
  87.9 45.6 %copy-start.5 = (f32[1024,256]{1,0:T(8,128)S(1)}, f32[1024,256]{1,0:T(8,128)}, u32[]{:S(2)}) copy-start(f32[1024,256]{1,0:T(8,128)} %param.9) | copy-start | bytes 3145732

commit v6 on v5

--- a/solution.py
+++ b/solution.py
@@ -64,7 +64,7 @@
     tokens, cols = blocks[0].shape
     me = lax.axis_index("tensor")
     for j, block in enumerate(blocks):
-        place = pl.multiple_of((me ^ j) * cols, cols)
+        place = pl.multiple_of((me % 2 ^ j) * cols, cols)
         columns_ref[:, pl.ds(place, cols)] = block[...]
     cot_top = functools.reduce(jnp.maximum, [top_of(block) for block in blocks])
     bound = jnp.maximum(top_ref[...] * cot_top * tokens, LEAST)
@@ -88,7 +88,7 @@
     )(features, own)
 
 
-def whole_columns(top, blocks):
+def pair_of_columns(top, blocks):
     one = jax.ShapeDtypeStruct((1, 1), F32)
     tokens, cols = blocks[0].shape
     columns, down, exponent = pl.pallas_call(
@@ -151,20 +151,27 @@
     total_cols = cols * tensor
     halves = dp // tensor
     part = rows // halves // replica
+    pair = 2
     run = halves * replica
     runs = [[t * dp * replica + i * run + s for s in range(run) for t in range(tensor)] for i in range(tensor)]
     apart = [[i * halves + h for i in range(tensor)] for h in range(halves)]
 
+    def messages(top, blocks):
+        columns, down, exponent = pair_of_columns(top, blocks)
+        partial = (contract_tokens(columns, features) * down).astype(LINK)
+        partial = partial.reshape(-1, TOLD, run, part).transpose(2, 0, 1, 3)
+        partial = partial.reshape(run, len(blocks), cols // TOLD, TOLD, part)
+        note = jnp.broadcast_to(exponent.astype(LINK), (run, len(blocks), 1, TOLD, part))
+        return jnp.concatenate([partial, note], axis=2)
+
     near, away = partner(cotangent, 1), partner(cotangent, 2)
     own, top = own_part(features, cotangent)
-    away, top = lax.optimization_barrier((away, top))
-    columns, down, exponent = whole_columns(top, [own, near, away, partner(away, 1)])
-
-    partial = (contract_tokens(columns, features) * down).astype(LINK)
-    partial = partial.reshape(total_cols // TOLD, TOLD, run, part).transpose(2, 0, 1, 3)
-    partial = partial.reshape(run, tensor, cols // TOLD, TOLD, part)
-    note = jnp.broadcast_to(exponent.astype(LINK), (run, tensor, 1, TOLD, part))
-    message = jnp.concatenate([partial, note], axis=2)
+    chip = lax.axis_index("tensor") // pair
+    message = jnp.zeros((run, pair, pair, cols // TOLD + 1, TOLD, part), LINK)
+    message = lax.dynamic_update_slice(message, messages(top, [own, near])[:, None], (0, chip, 0, 0, 0, 0))
+    away, message = lax.optimization_barrier((away, message))
+    far = messages(top, [away, partner(away, 1)])
+    message = lax.dynamic_update_slice(message, far[:, None], (0, 1 - chip, 0, 0, 0, 0))
     got = swap(message.reshape(run * tensor, cols + TOLD, part), EVERY, runs)
     got = got.reshape(run, tensor, cols + TOLD, part)
     factors = jnp.exp2(got[:, :, cols : cols + 1].astype(F32))

time: 136 us -> 135 us (level)
  Pallas kernels: 1.56 us -> 4.09 us
  waiting for transfers between devices: 5.31 us -> 2.81 us
  starting transfers between devices: 6.97 us -> 4.89 us
  blocking collectives: 107 us -> 105 us
  local copies, waits for them, and re-layouts: 4.86 us -> 6.36 us
    pallas_call x1 -> x2, Pallas kernels: 1.01 us -> 3.54 us  [pair_of_columns(): pl.pallas_call(columns_kernel, in_specs=[WHOLE] * (1 + len(blocks)), out_...]
    ppermute x3, waiting for transfers between devices: 5.31 us -> 2.81 us  [partner(): return lax.ppermute(x, 'tensor', [(i, i ^ bit) for i in range(count)])]
    ppermute x3, starting transfers between devices: 6.97 us -> 4.89 us  [partner(): return lax.ppermute(x, 'tensor', [(i, i ^ bit) for i in range(count)])]
    all_to_all x4, blocking collectives: 107 us -> 105 us  [swap(): lax.all_to_all(x, axis, split_axis=0, concat_axis=0, axis_index_groups=gr...]
    dot_general x1 -> x2, matrix products: 4.38 us -> 5.18 us  [contract_tokens(): lax.dot_general(left, right, (((0,), (0,)), ((), ())), preferred_element_...]
    unnamed x13 -> x19, local copies, waits for them, and re-layouts: 2.91 us -> 3.6 us
  transfers between devices with their start and end apart: 3 -> 3, of which waited for: 2 -> 2; matrix products, arithmetic and copies ran while one was open for 0% -> 3% of each run, Pallas kernels for 0% -> 2%
where the time goes in v6:
time: 135 us
  blocking collectives  105 us (78%)
  local copies, waits for them, and re-layouts  6.36 us (5%)
  matrix products  5.18 us (4%)
  starting transfers between devices  4.89 us (4%)
  Pallas kernels  4.09 us (3%)
  other arithmetic  3.92 us (3%)
  waiting for transfers between devices  2.81 us (2%)
  between operations  2.21 us (2%)
    all_to_all x4, blocking collectives, swap(): lax.all_to_all(x, axis, split_axis=0, concat_axis=0, axis_index_groups=gr...  105 us
    dot_general x2, matrix products, contract_tokens(): lax.dot_general(left, right, (((0,), (0,)), ((), ())), preferred_element_...  5.18 us
    ppermute x3, starting transfers between devices, partner(): return lax.ppermute(x, 'tensor', [(i, i ^ bit) for i in range(count)])  4.89 us
    unnamed x19, local copies, waits for them, and re-layouts  3.6 us
    pallas_call x2, Pallas kernels, pair_of_columns(): pl.pallas_call(columns_kernel, in_specs=[WHOLE] * (1 + len(blocks)), out_...  3.54 us
    ppermute x3, waiting for transfers between devices, partner(): return lax.ppermute(x, 'tensor', [(i, i ^ bit) for i in range(count)])  2.81 us
  transfers between devices with their start and end apart: 3, of which 2 were waited for; matrix products, arithmetic and copies ran while one was open for 3% of the time, Pallas kernels for 2%

profile of v6, /device:TPU:1, one launch (start us, length us, event | category | flops | bytes accessed | tf_op | source)
XLA Modules:
  0.0 134.6 jit_solution(15911418405418386723)
XLA Ops:
  0.6 3.3 %collective-permute-start.1 = (bf16[768,256]{1,0:T(8,128)(2,1)}, bf16[768,256]{1,0:T(8,128)(2,1)}, u32[]{:S(2)}, u32[]{:S(2)}) collective-permute-start(bf16[768,256]{1,0:T(8,128)(2,1)} %own_ref.1), channel_id=1, source_target_pairs={{0,64},{64,0},{128,192},{192,128},{1,65},{65,1},{129,193},{193,129... | collective-permute-start | bytes 1179656 | tf_op jit(solution)/shard_map/ppermute | solution.py:50
  4.0 1.2 collective-permute-start
  5.2 1.9 %copy-done = bf16[768,2048]{1,0:T(8,128)(2,1)S(1)} copy-done((bf16[768,2048]{1,0:T(8,128)(2,1)S(1)}, bf16[768,2048]{1,0:T(8,128)(2,1)}, u32[]{:S(2)}) %copy-start) | copy-done | bytes 3145752
  7.0 1.0 copy-done.2
  8.3 1.8 %columns.2 = (bf16[768,512]{1,0:T(8,128)(2,1)S(1)}, f32[1,1]{1,0:T(1,128)}, f32[1,1]{1,0:T(1,128)}) custom-call(f32[8,128]{1,0:T(8,128)S(1)} %get-tuple-element.13.top_ref, bf16[768,256]{1,0:T(8,128)(2,1)S(1)} %get-tuple-element.14.refs_0_, bf16[768,256]{1,0:T(8,128)(2,1)} %collective-permute-done.1.refs_1_), custom_call_target="tpu_custom_call" | custom-call | tf_op jit(solution)/shard_map/columns/pallas_call | solution.py:94
  10.2 2.5 %fusion = f16[16,64,8,128]{3,2,0,1:T(8,128)(2,1)S(1)} fusion(f32[]{:T(128)} %bitcast, bf16[768,512]{1,0:T(8,128)(2,1)S(1)} %get-tuple-element.15, bf16[768,2048]{1,0:T(8,128)(2,1)S(1)} %copy-done.1), kind=kOutput, calls=%fused_computation.5 | convolution fusion | flops 1612709888 | bytes 6029316 | tf_op jit(solution)/shard_map/dot_general | solution.py:35
  12.7 0.5 copy.10
  13.9 0.6 broadcast_in_dim.10
  14.5 0.6 bitcast_dynamic-update-slice_fusion.1
  15.0 1.3 collective-permute-done.refs_0_
  16.4 0.7 copy-done.3
  17.0 0.4 collective-permute-start.2
  17.4 1.5 %collective-permute-done.2.refs_1_ = bf16[768,256]{1,0:T(8,128)(2,1)} collective-permute-done((bf16[768,256]{1,0:T(8,128)(2,1)S(1)}, bf16[768,256]{1,0:T(8,128)(2,1)}, u32[]{:S(2)}, u32[]{:S(2)}) %collective-permute-start.2) | collective-permute-done | bytes 393248 | tf_op jit(solution)/shard_map/ppermute | solution.py:50
  18.9 1.7 %columns.3 = (bf16[768,512]{1,0:T(8,128)(2,1)S(1)}, f32[1,1]{1,0:T(1,128)}, f32[1,1]{1,0:T(1,128)}) custom-call(f32[8,128]{1,0:T(8,128)S(1)} %get-tuple-element.13.top_ref, bf16[768,256]{1,0:T(8,128)(2,1)S(1)} %collective-permute-done.refs_0_, bf16[768,256]{1,0:T(8,128)(2,1)} %collective-permute-done.2.refs_1_), custom_call_target="tpu_custom_call" | custom-call | tf_op jit(solution)/shard_map/columns/pallas_call | solution.py:94
  20.6 2.7 %fusion.1 = f16[16,64,8,128]{3,2,0,1:T(8,128)(2,1)S(1)} fusion(f32[]{:T(128)} %bitcast.6, bf16[768,512]{1,0:T(8,128)(2,1)S(1)} %get-tuple-element.20, bf16[768,2048]{1,0:T(8,128)(2,1)S(1)} %copy-done.1), kind=kOutput, calls=%fused_computation.6 | convolution fusion | flops 1612709888 | bytes 6029316 | tf_op jit(solution)/shard_map/dot_general | solution.py:35
  23.3 0.5 copy.11
  24.5 0.6 bitcast_dynamic-update-slice_fusion
  25.0 60.7 %all_to_all.20 = f16[64,264,128]{2,1,0:T(8,128)(2,1)S(1)} all-to-all(f16[64,264,128]{2,1,0:T(8,128)(2,1)S(1)} %bitcast.39), channel_id=1, replica_groups={{0,64,128,192,1,65,129,193,2,66,130,194,3,67,131,195,4,68,132,196,5,69,..., dimensions={0} | all-to-all | bytes 8650752 | tf_op jit(solution)/shard_map/all_to_all | solution.py:41
  85.8 0.9 multiply_reduce_fusion
  86.9 17.0 %all_to_all.21 = f16[4,264,128]{2,1,0:T(8,128)(2,1)S(1)} all-to-all(f16[4,264,128]{2,1,0:T(8,128)(2,1)S(1)} %pad_maximum_fusion), channel_id=1, replica_groups={{0,16,32,48},{8,24,40,56},{1,17,33,49},{9,25,41,57},{2,18,34,50},{10,26..., dimensions={0} | all-to-all | bytes 540672 | tf_op jit(solution)/shard_map/all_to_all | solution.py:41
  104.2 15.3 %all_to_all.22.squares_ref = f32[32,1,128]{2,1,0:T(1,128)S(1)} all-to-all(f32[32,1,128]{2,1,0:T(1,128)S(1)} %squares.1), channel_id=1, replica_groups=mesh['tensor'=4,'dp'=8,'replica'=8] {'tensor','dp'}, dimensions={0} | all-to-all | bytes 32768 | tf_op jit(solution)/shard_map/all_to_all | solution.py:41
  119.6 12.2 %all_to_all.23 = f16[8,136,256]{2,1,0:T(8,128)(2,1)S(1)} all-to-all(f16[8,136,256]{2,1,0:T(8,128)(2,1)S(1)} %broadcast_in_dim.26), channel_id=1, replica_groups=mesh['tensor'=4,'dp'=8,'replica'=8] {'replica'}, dimensions={0} | all-to-all | bytes 1114112 | tf_op jit(solution)/shard_map/all_to_all | solution.py:41
  132.0 0.4 negate_select_fusion
  132.4 2.2 %multiply_subtract_fusion = (f32[1024,256]{1,0:T(8,128)}, f32[1024,256]{1,0:T(8,128)}, f32[1024,256]{1,0:T(8,128)}) fusion(f32[1024,256]{1,0:T(8,128)S(1)} %copy-done.4, f32[8,128,256]{2,1,0:T(8,128)S(1)} %negate_select_fusion, f32[256]{0:T(256)S(1)} %rsqrt_minimum_fusion, f32[1024,256]{1,0:T(8,128)S(1)} %copy-done.5, f32[1024,256]{1,0:T(8,128)S(1)} %copy-done.6), kind=kLoop, calls=%fused_computation.11 | loop fusion | flops 4194304 | bytes 7341056 | tf_op jit(solution)/shard_map/sub | solution.py:201
  (34 shorter events, 1.1 us)
Async XLA Ops:
  0.6 7.7 %collective-permute-start.1 = (bf16[768,256]{1,0:T(8,128)(2,1)}, bf16[768,256]{1,0:T(8,128)(2,1)}, u32[]{:S(2)}, u32[]{:S(2)}) collective-permute-start(bf16[768,256]{1,0:T(8,128)(2,1)} %own_ref.1), channel_id=1, source_target_pairs={{0,64},{64,0},{128,192},{192,128},{1,65},{65,1},{129,193},{193,129... | collective-permute-start | bytes 1179656 | tf_op jit(solution)/shard_map/ppermute | solution.py:50
  4.0 12.4 %collective-permute-start = (bf16[768,256]{1,0:T(8,128)(2,1)}, bf16[768,256]{1,0:T(8,128)(2,1)S(1)}, u32[]{:S(2)}, u32[]{:S(2)}) collective-permute-start(bf16[768,256]{1,0:T(8,128)(2,1)} %own_ref.1), channel_id=1, source_target_pairs={{0,128},{64,192},{128,0},{192,64},{1,129},{65,193},{129,1},{193,65... | collective-permute-start | bytes 1179656 | tf_op jit(solution)/shard_map/ppermute | solution.py:50
  5.2 1.9 %copy-start = (bf16[768,2048]{1,0:T(8,128)(2,1)S(1)}, bf16[768,2048]{1,0:T(8,128)(2,1)}, u32[]{:S(2)}) copy-start(bf16[768,2048]{1,0:T(8,128)(2,1)} %features_ref.1) | copy-start | bytes 9437188
  7.0 1.0 copy-start.2
  8.0 2.2 %copy-start.1 = (bf16[768,2048]{1,0:T(8,128)(2,1)S(1)}, bf16[768,2048]{1,0:T(8,128)(2,1)}, u32[]{:S(2)}) copy-start(bf16[768,2048]{1,0:T(8,128)(2,1)} %features_ref.1) | copy-start | bytes 9437188
  15.0 2.0 %copy-start.3 = (f16[16,2,2,33,8,128]{5,4,3,2,1,0:T(8,128)(2,1)}, f16[16,2,2,33,8,128]{5,4,3,2,1,0:T(8,128)(2,1)S(1)}, u32[]{:S(2)}) copy-start(f16[16,2,2,33,8,128]{5,4,3,2,1,0:T(8,128)(2,1)S(1)} %bitcast_dynamic-update-slice_fusion.1) | copy-start | bytes 12976132
  17.0 1.9 %collective-permute-start.2 = (bf16[768,256]{1,0:T(8,128)(2,1)S(1)}, bf16[768,256]{1,0:T(8,128)(2,1)}, u32[]{:S(2)}, u32[]{:S(2)}) collective-permute-start(bf16[768,256]{1,0:T(8,128)(2,1)S(1)} %collective-permute-done.refs_0_), channel_id=1, source_target_pairs={{0,64},{64,0},{128,192},{192,128},{1,65},{65,1},{129,193},{193,129... | collective-permute-start | bytes 1179656 | tf_op jit(solution)/shard_map/ppermute | solution.py:50
  20.6 3.8 %slice-start = ((s8[4325376]{0:T(1024)(128)(4,1)}), s8[4194304]{0:T(1024)(128)(4,1)S(1)}, s32[]{:S(2)}) async-start(s8[4325376]{0:T(1024)(128)(4,1)} %bitcast.37), calls=%async_computation.4 | async-start | bytes 8388608
  20.6 3.9 %slice-start.1 = ((s8[4325376]{0:T(1024)(128)(4,1)}), s8[131072]{0:T(1024)(128)(4,1)S(1)}, s32[]{:S(2)}) async-start(s8[4325376]{0:T(1024)(128)(4,1)} %bitcast.37), calls=%async_computation.5 | async-start | bytes 262144
  86.8 45.6 %copy-start.4 = (f32[1024,256]{1,0:T(8,128)S(1)}, f32[1024,256]{1,0:T(8,128)}, u32[]{:S(2)}) copy-start(f32[1024,256]{1,0:T(8,128)} %param.7) | copy-start | bytes 3145732
  86.8 45.6 %copy-start.5 = (f32[1024,256]{1,0:T(8,128)S(1)}, f32[1024,256]{1,0:T(8,128)}, u32[]{:S(2)}) copy-start(f32[1024,256]{1,0:T(8,128)} %param.8) | copy-start | bytes 3145732
  86.9 45.6 %copy-start.6 = (f32[1024,256]{1,0:T(8,128)S(1)}, f32[1024,256]{1,0:T(8,128)}, u32[]{:S(2)}) copy-start(f32[1024,256]{1,0:T(8,128)} %param.9) | copy-start | bytes 3145732

commit v7 on v6

--- a/solution.py
+++ b/solution.py
@@ -153,13 +153,13 @@
     part = rows // halves // replica
     pair = 2
     run = halves * replica
-    runs = [[t * dp * replica + i * run + s for s in range(run) for t in range(tensor)] for i in range(tensor)]
+    runs = [[t * dp * replica + i * run + h * replica + r for r in range(replica) for h in range(halves) for t in range(tensor)] for i in range(tensor)]
     apart = [[i * halves + h for i in range(tensor)] for h in range(halves)]
 
     def messages(top, blocks):
         columns, down, exponent = pair_of_columns(top, blocks)
         partial = (contract_tokens(columns, features) * down).astype(LINK)
-        partial = partial.reshape(-1, TOLD, run, part).transpose(2, 0, 1, 3)
+        partial = partial.reshape(-1, TOLD, halves, replica, part).transpose(3, 2, 0, 1, 4)
         partial = partial.reshape(run, len(blocks), cols // TOLD, TOLD, part)
         note = jnp.broadcast_to(exponent.astype(LINK), (run, len(blocks), 1, TOLD, part))
         return jnp.concatenate([partial, note], axis=2)

time: 135 us -> 135 us (level)
  no operation moved by 1% of the time
where the time goes in v7:
time: 135 us; the launch traced here: 134 us
  blocking collectives  105 us (78%)
  local copies, waits for them, and re-layouts  6.32 us (5%)
  matrix products  5.1 us (4%)
  starting transfers between devices  4.89 us (4%)
  Pallas kernels  4.09 us (3%)
  other arithmetic  3.92 us (3%)
  waiting for transfers between devices  2.85 us (2%)
  between operations  2.21 us (2%)
    all_to_all x4, blocking collectives, swap(): lax.all_to_all(x, axis, split_axis=0, concat_axis=0, axis_index_groups=gr...  105 us
    dot_general x2, matrix products, contract_tokens(): lax.dot_general(left, right, (((0,), (0,)), ((), ())), preferred_element_...  5.1 us
    ppermute x3, starting transfers between devices, partner(): return lax.ppermute(x, 'tensor', [(i, i ^ bit) for i in range(count)])  4.89 us
    unnamed x19, local copies, waits for them, and re-layouts  3.56 us
    pallas_call x2, Pallas kernels, pair_of_columns(): pl.pallas_call(columns_kernel, in_specs=[WHOLE] * (1 + len(blocks)), out_...  3.54 us
    ppermute x3, waiting for transfers between devices, partner(): return lax.ppermute(x, 'tensor', [(i, i ^ bit) for i in range(count)])  2.85 us
  transfers between devices with their start and end apart: 3, of which 2 were waited for; matrix products, arithmetic and copies ran while one was open for 3% of the time, Pallas kernels for 2%

profile of v7, /device:TPU:1, one launch (start us, length us, event | category | flops | bytes accessed | tf_op | source)
XLA Modules:
  0.0 134.4 jit_solution(8109689636768892194)
XLA Ops:
  0.6 3.3 %collective-permute-start.1 = (bf16[768,256]{1,0:T(8,128)(2,1)}, bf16[768,256]{1,0:T(8,128)(2,1)}, u32[]{:S(2)}, u32[]{:S(2)}) collective-permute-start(bf16[768,256]{1,0:T(8,128)(2,1)} %own_ref.1), channel_id=1, source_target_pairs={{0,64},{64,0},{128,192},{192,128},{1,65},{65,1},{129,193},{193,129... | collective-permute-start | bytes 1179656 | tf_op jit(solution)/shard_map/ppermute | solution.py:50
  4.0 1.2 collective-permute-start
  5.2 1.9 %copy-done = bf16[768,2048]{1,0:T(8,128)(2,1)S(1)} copy-done((bf16[768,2048]{1,0:T(8,128)(2,1)S(1)}, bf16[768,2048]{1,0:T(8,128)(2,1)}, u32[]{:S(2)}) %copy-start) | copy-done | bytes 3145752
  7.0 1.0 copy-done.2
  8.3 1.8 %columns.2 = (bf16[768,512]{1,0:T(8,128)(2,1)S(1)}, f32[1,1]{1,0:T(1,128)}, f32[1,1]{1,0:T(1,128)}) custom-call(f32[8,128]{1,0:T(8,128)S(1)} %get-tuple-element.13.top_ref, bf16[768,256]{1,0:T(8,128)(2,1)S(1)} %get-tuple-element.14.refs_0_, bf16[768,256]{1,0:T(8,128)(2,1)} %collective-permute-done.1.refs_1_), custom_call_target="tpu_custom_call" | custom-call | tf_op jit(solution)/shard_map/columns/pallas_call | solution.py:94
  10.2 2.5 %multiply_convert_fusion.1 = f16[512,2048]{1,0:T(8,128)(2,1)S(1)} fusion(bf16[768,512]{1,0:T(8,128)(2,1)S(1)} %get-tuple-element.15, bf16[768,2048]{1,0:T(8,128)(2,1)S(1)} %copy-done.1, f32[]{:T(128)} %bitcast), kind=kOutput, calls=%fused_computation.2 | convolution fusion | flops 1612709888 | bytes 6029316 | tf_op jit(solution)/shard_map/dot_general | solution.py:35
  12.7 0.5 copy.14
  13.8 0.6 broadcast_in_dim.10
  14.4 0.6 bitcast_dynamic-update-slice_fusion.1
  15.0 1.4 %collective-permute-done.refs_0_ = bf16[768,256]{1,0:T(8,128)(2,1)S(1)} collective-permute-done((bf16[768,256]{1,0:T(8,128)(2,1)}, bf16[768,256]{1,0:T(8,128)(2,1)S(1)}, u32[]{:S(2)}, u32[]{:S(2)}) %collective-permute-start) | collective-permute-done | bytes 393248 | tf_op jit(solution)/shard_map/ppermute | solution.py:50
  16.4 0.6 copy-done.3
  17.0 0.4 collective-permute-start.2
  17.4 1.5 %collective-permute-done.2.refs_1_ = bf16[768,256]{1,0:T(8,128)(2,1)} collective-permute-done((bf16[768,256]{1,0:T(8,128)(2,1)S(1)}, bf16[768,256]{1,0:T(8,128)(2,1)}, u32[]{:S(2)}, u32[]{:S(2)}) %collective-permute-start.2) | collective-permute-done | bytes 393248 | tf_op jit(solution)/shard_map/ppermute | solution.py:50
  18.8 1.7 %columns.3 = (bf16[768,512]{1,0:T(8,128)(2,1)S(1)}, f32[1,1]{1,0:T(1,128)}, f32[1,1]{1,0:T(1,128)}) custom-call(f32[8,128]{1,0:T(8,128)S(1)} %get-tuple-element.13.top_ref, bf16[768,256]{1,0:T(8,128)(2,1)S(1)} %collective-permute-done.refs_0_, bf16[768,256]{1,0:T(8,128)(2,1)} %collective-permute-done.2.refs_1_), custom_call_target="tpu_custom_call" | custom-call | tf_op jit(solution)/shard_map/columns/pallas_call | solution.py:94
  20.5 2.6 %multiply_convert_fusion = f16[512,2048]{1,0:T(8,128)(2,1)S(1)} fusion(bf16[768,512]{1,0:T(8,128)(2,1)S(1)} %get-tuple-element.20, bf16[768,2048]{1,0:T(8,128)(2,1)S(1)} %copy-done.1, f32[]{:T(128)} %bitcast.7), kind=kOutput, calls=%fused_computation.1 | convolution fusion | flops 1612709888 | bytes 6029316 | tf_op jit(solution)/shard_map/dot_general | solution.py:35
  23.2 0.5 copy.16
  24.4 0.6 bitcast_dynamic-update-slice_fusion
  25.0 60.6 %all_to_all.20 = f16[64,264,128]{2,1,0:T(8,128)(2,1)S(1)} all-to-all(f16[64,264,128]{2,1,0:T(8,128)(2,1)S(1)} %bitcast.41), channel_id=1, replica_groups={{0,64,128,192,8,72,136,200,1,65,129,193,9,73,137,201,2,66,130,194,10,74..., dimensions={0} | all-to-all | bytes 8650752 | tf_op jit(solution)/shard_map/all_to_all | solution.py:41
  85.7 0.9 multiply_reduce_fusion
  86.7 17.3 %all_to_all.21 = f16[4,264,128]{2,1,0:T(8,128)(2,1)S(1)} all-to-all(f16[4,264,128]{2,1,0:T(8,128)(2,1)S(1)} %pad_maximum_fusion), channel_id=1, replica_groups={{0,16,32,48},{8,24,40,56},{1,17,33,49},{9,25,41,57},{2,18,34,50},{10,26..., dimensions={0} | all-to-all | bytes 540672 | tf_op jit(solution)/shard_map/all_to_all | solution.py:41
  104.4 14.8 %all_to_all.22.squares_ref = f32[32,1,128]{2,1,0:T(1,128)S(1)} all-to-all(f32[32,1,128]{2,1,0:T(1,128)S(1)} %squares.1), channel_id=1, replica_groups=mesh['tensor'=4,'dp'=8,'replica'=8] {'tensor','dp'}, dimensions={0} | all-to-all | bytes 32768 | tf_op jit(solution)/shard_map/all_to_all | solution.py:41
  119.3 12.3 %all_to_all.23 = f16[8,136,256]{2,1,0:T(8,128)(2,1)S(1)} all-to-all(f16[8,136,256]{2,1,0:T(8,128)(2,1)S(1)} %broadcast_in_dim.26), channel_id=1, replica_groups=mesh['tensor'=4,'dp'=8,'replica'=8] {'replica'}, dimensions={0} | all-to-all | bytes 1114112 | tf_op jit(solution)/shard_map/all_to_all | solution.py:41
  131.7 0.4 negate_select_fusion
  132.2 2.2 %multiply_subtract_fusion = (f32[1024,256]{1,0:T(8,128)}, f32[1024,256]{1,0:T(8,128)}, f32[1024,256]{1,0:T(8,128)}) fusion(f32[1024,256]{1,0:T(8,128)S(1)} %copy-done.4, f32[8,128,256]{2,1,0:T(8,128)S(1)} %negate_select_fusion, f32[256]{0:T(256)S(1)} %rsqrt_minimum_fusion, f32[1024,256]{1,0:T(8,128)S(1)} %copy-done.5, f32[1024,256]{1,0:T(8,128)S(1)} %copy-done.6), kind=kLoop, calls=%fused_computation.9 | loop fusion | flops 4194304 | bytes 7341056 | tf_op jit(solution)/shard_map/sub | solution.py:201
  (34 shorter events, 1.1 us)
Async XLA Ops:
  0.6 7.7 %collective-permute-start.1 = (bf16[768,256]{1,0:T(8,128)(2,1)}, bf16[768,256]{1,0:T(8,128)(2,1)}, u32[]{:S(2)}, u32[]{:S(2)}) collective-permute-start(bf16[768,256]{1,0:T(8,128)(2,1)} %own_ref.1), channel_id=1, source_target_pairs={{0,64},{64,0},{128,192},{192,128},{1,65},{65,1},{129,193},{193,129... | collective-permute-start | bytes 1179656 | tf_op jit(solution)/shard_map/ppermute | solution.py:50
  4.0 12.4 %collective-permute-start = (bf16[768,256]{1,0:T(8,128)(2,1)}, bf16[768,256]{1,0:T(8,128)(2,1)S(1)}, u32[]{:S(2)}, u32[]{:S(2)}) collective-permute-start(bf16[768,256]{1,0:T(8,128)(2,1)} %own_ref.1), channel_id=1, source_target_pairs={{0,128},{64,192},{128,0},{192,64},{1,129},{65,193},{129,1},{193,65... | collective-permute-start | bytes 1179656 | tf_op jit(solution)/shard_map/ppermute | solution.py:50
  5.2 1.9 %copy-start = (bf16[768,2048]{1,0:T(8,128)(2,1)S(1)}, bf16[768,2048]{1,0:T(8,128)(2,1)}, u32[]{:S(2)}) copy-start(bf16[768,2048]{1,0:T(8,128)(2,1)} %features_ref.1) | copy-start | bytes 9437188
  7.0 1.0 copy-start.2
  8.0 2.2 %copy-start.1 = (bf16[768,2048]{1,0:T(8,128)(2,1)S(1)}, bf16[768,2048]{1,0:T(8,128)(2,1)}, u32[]{:S(2)}) copy-start(bf16[768,2048]{1,0:T(8,128)(2,1)} %features_ref.1) | copy-start | bytes 9437188
  15.0 2.0 %copy-start.3 = (f16[16,2,2,33,8,128]{5,4,3,2,1,0:T(8,128)(2,1)}, f16[16,2,2,33,8,128]{5,4,3,2,1,0:T(8,128)(2,1)S(1)}, u32[]{:S(2)}) copy-start(f16[16,2,2,33,8,128]{5,4,3,2,1,0:T(8,128)(2,1)S(1)} %bitcast_dynamic-update-slice_fusion.1) | copy-start | bytes 12976132
  17.0 1.9 %collective-permute-start.2 = (bf16[768,256]{1,0:T(8,128)(2,1)S(1)}, bf16[768,256]{1,0:T(8,128)(2,1)}, u32[]{:S(2)}, u32[]{:S(2)}) collective-permute-start(bf16[768,256]{1,0:T(8,128)(2,1)S(1)} %collective-permute-done.refs_0_), channel_id=1, source_target_pairs={{0,64},{64,0},{128,192},{192,128},{1,65},{65,1},{129,193},{193,129... | collective-permute-start | bytes 1179656 | tf_op jit(solution)/shard_map/ppermute | solution.py:50
  20.5 3.8 %slice-start = ((s8[4325376]{0:T(1024)(128)(4,1)}), s8[4194304]{0:T(1024)(128)(4,1)S(1)}, s32[]{:S(2)}) async-start(s8[4325376]{0:T(1024)(128)(4,1)} %bitcast.39), calls=%async_computation.4 | async-start | bytes 8388608
  20.5 3.8 %slice-start.1 = ((s8[4325376]{0:T(1024)(128)(4,1)}), s8[131072]{0:T(1024)(128)(4,1)S(1)}, s32[]{:S(2)}) async-start(s8[4325376]{0:T(1024)(128)(4,1)} %bitcast.39), calls=%async_computation.5 | async-start | bytes 262144
  86.7 45.5 %copy-start.4 = (f32[1024,256]{1,0:T(8,128)S(1)}, f32[1024,256]{1,0:T(8,128)}, u32[]{:S(2)}) copy-start(f32[1024,256]{1,0:T(8,128)} %param.7) | copy-start | bytes 3145732
  86.7 45.5 %copy-start.5 = (f32[1024,256]{1,0:T(8,128)S(1)}, f32[1024,256]{1,0:T(8,128)}, u32[]{:S(2)}) copy-start(f32[1024,256]{1,0:T(8,128)} %param.8) | copy-start | bytes 3145732
  86.7 45.5 %copy-start.6 = (f32[1024,256]{1,0:T(8,128)S(1)}, f32[1024,256]{1,0:T(8,128)}, u32[]{:S(2)}) copy-start(f32[1024,256]{1,0:T(8,128)} %param.9) | copy-start | bytes 3145732
